TPU v7x, 32 devices: a whole 2x2x4 slice. The times are simulated.
32 devices in a mesh: win: 2 (over y), row: 16 (over z, x, core).
Axes of the slice: x: 2, y: 2, z: 4, core: 2. Of those that a mesh axis runs over, the one named last changes fastest.
Arguments:
- image: float32 [3, 2048, 4096], P(None, ('win', 'row')), parts along dimension 1, may hold values from -6 to 6
- grad_x: bfloat16 [3, 2048, 4096], P(None, ('win', 'row')), parts along dimension 1, may hold values from -6 to 6
- grad_y: bfloat16 [3, 2048, 4096], P(None, ('win', 'row')), parts along dimension 1, may hold values from -6 to 6
- classes: int32 [2048, 4096], P(('win', 'row')), parts along dimension 0, may hold values from 0 to 3
- validity: int32 [2, 4], P('win'), parts along dimension 0, may hold values 0 or 1
- owners: int32 [2, 4, 2], P('win'), parts along dimension 0, may hold values from 0 to 1
Outputs:
- solution: float32 [3, 2048, 4096], P(None, ('win', 'row')), parts along dimension 1
There are 2 independent parts, one for each index of `win`. A program takes and returns all parts, laid end to end along the dimension named above; each array names one. Nothing has to cross between parts.
All inputs are finite; a program needn't handle non-finite values.
Results may differ from a plain program's by a relative error of at most 0.0003.
Values may be sent and summed in bfloat16 or wider, within the bound.
A program may use at most 128 MiB of HBM per device.

v0:
```python
import jax
import jax.numpy as jnp
from jax import lax
from jax.sharding import PartitionSpec as P

TILE_ROWS = 1024
TILE_COLS = 1024
TILES_X = 4
BAND = 48
SWEEPS = 4
WIDTH = 4096


OMEGA = 0.8
SCREEN = 0.25


def passed_along(x, axis, by):
    devices = lax.axis_size(axis)
    pairs = [(i, i + by) for i in range(devices) if 0 <= i + by < devices]
    return lax.ppermute(x, axis, pairs)


def carried_in(x, axis, combine, identity):
    devices, position = (lax.axis_size(axis), lax.axis_index(axis))
    everything = jax.tree.map(lambda part: lax.all_gather(part, axis), x)
    start = jax.tree.map(
        lambda part, zero: jnp.broadcast_to(jnp.asarray(zero, part.dtype), part.shape), x, identity
    )

    def turn(k, before):
        reached = k < position
        new = combine(before, jax.tree.map(lambda part: part[k], everything))
        return jax.tree.map(lambda a, b: jnp.where(reached, a, b), new, before)

    return lax.fori_loop(0, devices, turn, start)


def with_halo(block, sides, width):
    for axis, dim in sides:
        count = lax.axis_size(axis)
        forward = [(i, i + 1) for i in range(count - 1)]
        backward = [(target, source) for source, target in forward]
        low = lax.ppermute(
            lax.slice_in_dim(block, block.shape[dim] - width, None, axis=dim), axis, forward
        )
        high = lax.ppermute(lax.slice_in_dim(block, 0, width, axis=dim), axis, backward)
        block = jnp.concatenate([low, block, high], axis=dim)
    return block


def divergence(horiz_pad, vert_pad):
    horiz_here = horiz_pad[:, 1:, 1:-1]
    horiz_left = horiz_pad[:, 1:, :-2]
    horiz_above = horiz_pad[:, :-1, 1:-1]
    horiz_corner = horiz_pad[:, :-1, :-2]
    vert_here = vert_pad[:, 1:, 1:-1]
    vert_right = vert_pad[:, 1:, 2:]
    vert_left = vert_pad[:, 1:, :-2]
    vert_above = vert_pad[:, :-1, 1:-1]
    diagonal = (
        horiz_here
        + vert_right
        - horiz_corner
        - vert_above
        + vert_left
        - horiz_left
        - vert_above
        + horiz_above
    )
    return horiz_here - horiz_left + vert_here - vert_above + 0.5 * diagonal


def neighbours(padded):
    axial = padded[:, :-2, 1:-1] + padded[:, 2:, 1:-1] + padded[:, 1:-1, :-2] + padded[:, 1:-1, 2:]
    corner = padded[:, :-2, :-2] + padded[:, :-2, 2:] + padded[:, 2:, :-2] + padded[:, 2:, 2:]
    return axial + 0.5 * corner


def relax(row_padded, target, div_term, weights):
    current = row_padded[:, 1:-1, :]
    padded = jnp.pad(row_padded, ((0, 0), (0, 0), (1, 1)))
    return (1.0 - OMEGA) * current + OMEGA * (weights * target + neighbours(padded) - div_term) / (
        weights + 6.0
    )


def join_prefix(earlier, later):
    return (
        earlier[0] + later[0],
        jnp.where(earlier[2] > 0, earlier[1], later[1]),
        jnp.maximum(earlier[2], later[2]),
    )


def per_device(image, grad_x, grad_y, classes, validity, owners):
    band_rows = image.shape[1]
    devices = lax.axis_size("row")
    position = lax.axis_index("row")
    first_row = position * band_rows
    horizontal = grad_x.astype(jnp.float32)
    vertical = grad_y.astype(jnp.float32)
    tile_row = first_row // TILE_ROWS
    own_row = lax.dynamic_index_in_dim(owners, tile_row, 0, keepdims=False)
    lower_mean = passed_along(
        jnp.mean(vertical[:, :BAND, :], axis=1).astype(jnp.bfloat16), "row", -1
    ).astype(jnp.float32)
    upper_mean = jnp.mean(vertical[:, band_rows - 1 - BAND : band_rows - 1, :], axis=1)
    lower_owns = jnp.repeat(own_row[:, 0], TILE_COLS, total_repeat_length=WIDTH)[None] == 1
    at_seam = ((first_row + band_rows) % TILE_ROWS == 0) & (position < devices - 1)
    last_row = jnp.where(at_seam, jnp.where(lower_owns, lower_mean, upper_mean), vertical[:, -1, :])
    vertical = vertical.at[:, -1, :].set(last_row)
    horiz_tiles = horizontal.reshape(3, band_rows, TILES_X, TILE_COLS)
    left_mean = jnp.mean(horiz_tiles[:, :, :-1, TILE_COLS - 1 - BAND : TILE_COLS - 1], axis=3)
    right_mean = jnp.mean(horiz_tiles[:, :, 1:, :BAND], axis=3)
    right_owns = (own_row[:-1, 1] == 1)[None, None, :]
    horiz_tiles = horiz_tiles.at[:, :, :-1, TILE_COLS - 1].set(
        jnp.where(right_owns, right_mean, left_mean)
    )
    horizontal = horiz_tiles.reshape(3, band_rows, WIDTH)
    above_horiz, above_vert = (
        passed_along(horizontal[:, -1:, :].astype(jnp.bfloat16), "row", 1).astype(jnp.float32),
        passed_along(vertical[:, -1:, :].astype(jnp.bfloat16), "row", 1).astype(jnp.float32),
    )
    column_pad = ((0, 0), (0, 0), (1, 1))
    div_term = divergence(
        jnp.pad(jnp.concatenate([above_horiz, horizontal], axis=1), column_pad),
        jnp.pad(jnp.concatenate([above_vert, vertical], axis=1), column_pad),
    )
    mean_vert = jnp.mean(vertical, axis=2)
    mean_image = jnp.mean(image, axis=2)
    running = jnp.cumsum(mean_vert, axis=1) - mean_vert
    totals = jnp.sum(mean_vert, axis=1)
    leading = mean_image[:, 0]
    empty_three = jnp.zeros((3,), jnp.float32)
    before, prior_first, prior_seen = carried_in(
        (totals, leading, jnp.ones((1,), jnp.float32)),
        "row",
        join_prefix,
        (empty_three, empty_three, jnp.zeros((1,), jnp.float32)),
    )
    window_first = jnp.where(prior_seen > 0, prior_first, leading)
    level = before[:, None] + running - mean_image + window_first[:, None]
    target = image + level[:, :, None]
    cover = jnp.repeat(
        lax.dynamic_index_in_dim(validity, tile_row, 0, keepdims=False),
        TILE_COLS,
        total_repeat_length=WIDTH,
    ).astype(jnp.float32)
    weights = cover[None, :] * SCREEN * jnp.exp2(classes.astype(jnp.float32))
    solution = target
    for sweep in range(SWEEPS):
        row_padded = with_halo(solution, (("row", 1),), 1)
        solution = relax(row_padded, target, div_term, weights)
    return solution


def solution(mesh):
    in_specs = (
        P(None, ("win", "row"), None),
        P(None, ("win", "row"), None),
        P(None, ("win", "row"), None),
        P(("win", "row"), None),
        P("win", None),
        P("win", None, None),
    )
    out_specs = P(None, ("win", "row"), None)
    return jax.shard_map(
        per_device, mesh=mesh, in_specs=in_specs, out_specs=out_specs, check_vma=False
    )
```

profile of v0, /device:TPU:1, one launch (start us, length us, event | category | flops | bytes accessed | tf_op | source)
XLA Modules:
  0.0 210.6 jit_solution(10474253459395637235)
XLA Ops:
  1.3 5.1 %reshape.222 = f32[3,64,4,1024]{3,2,1,0:T(4,128)} reshape(bf16[3,64,4096]{2,1,0:T(8,128)(2,1)} %param.19) | data formatting | bytes 4718592 | tf_op jit(solution)/shard_map/reshape | solution.py:113
  9.7 3.2 %dynamic-slice_select_fusion = f32[3,64,3,1]{3,2,1,0:T(4,128)S(1)} fusion(f32[3,64,4,1024]{3,2,1,0:T(4,128)} %reshape.222, s32[]{:T(128)} %bitcast.19, s32[]{:T(128)} %bitcast.20, f32[3,64,3,1]{3,2,1,0:T(4,128)S(1)} %copy.31, f32[3,64,3,1]{3,2,1,0:T(4,128)S(1)} %copy.32, pred[3]{0:T(512)(128)(4,1)S(1)} %compare_bitcast_fusion, pred[]{:T(512)} %and_reduce_fusion), kind=kLoop, calls=%fused_computation.109 | loop fusion | flops 1152 | bytes 9228 | tf_op jit(solution)/shard_map/select.6
  12.9 34.4 %scatter.9 = f32[3,64,4,1024]{3,2,1,0:T(4,128)} dynamic-update-slice(f32[3,64,4,1024]{3,2,1,0:T(4,128)} %reshape.222, f32[3,64,3,1]{3,2,1,0:T(4,128)S(1)} %dynamic-slice_select_fusion, s32[]{:T(128)} %constant.225.clone.1, s32[]{:T(128)} %constant.225.clone.1, s32[]{:T(128)} %bitcast.19, s32[]{:T(128)} %bitcast.20) | dynamic-update-slice | bytes 4612 | tf_op jit(solution)/shard_map/scatter | solution.py:117
  47.4 3.9 %reshape.220 = f32[3,64,4096]{2,1,0:T(8,128)S(1)} reshape(f32[3,64,4,1024]{3,2,1,0:T(4,128)} %scatter.9) | data formatting | bytes 6291456 | tf_op jit(solution)/shard_map/reshape | solution.py:120
  53.0 4.5 %collective-permute-start.3 = (bf16[3,1,4096]{2,1,0:T(2,128)(2,1)S(1)}, bf16[3,1,4096]{2,1,0:T(2,128)(2,1)S(1)}, u32[]{:S(2)}, u32[]{:S(2)}) collective-permute-start(bf16[3,1,4096]{2,1,0:T(2,128)(2,1)S(1)} %slice.552), channel_id=1, source_target_pairs={{0,1},{1,2},{2,3},{3,4},{4,5},{5,6},{6,7},{7,8},{8,9},{9,10},{10,1... | collective-permute-start | bytes 73736 | tf_op jit(solution)/shard_map/ppermute | solution.py:21
  59.9 1.9 collective-permute-start
  62.5 2.1 %reduce_sum.67 = f32[3,64]{1,0:T(4,128)S(1)} reduce(f32[3,64,4096]{2,1,0:T(8,128)} %param.18, f32[]{:T(128)} %constant.226.clone.1), dimensions={2}, to_apply=%region_4.6 | reduce | flops 786240 | bytes 3146500 | tf_op jit(solution)/shard_map/reduce_sum | solution.py:131
  65.3 2.5 %fusion.46 = f32[4096]{0:T(1024)S(1)} fusion(pred[4096]{0:T(1024)(128)(4,1)S(1)} %copy-done.9, pred[4096]{0:T(1024)(128)(4,1)S(1)} %copy-done.8, pred[4096]{0:T(1024)(128)(4,1)S(1)} %copy-done.7, s32[]{:T(128)} %bitcast.15, s32[]{:T(128)} %bitcast.14, s32[]{:T(128)} %bitcast.13, s32[]{:T(128)} %bitcast.12), kind=kLoop, calls=%fused_computation.117 | loop fusion | flops 20480 | bytes 28688 | tf_op jit(solution)/shard_map/mul | solution.py:150
  67.7 2.8 %broadcast_add_fusion.1 = (f32[64,4096]{1,0:T(8,128)}, f32[64,4096]{1,0:T(8,128)}) fusion(s32[64,4096]{1,0:T(8,128)} %param.21, f32[4096]{0:T(1024)S(1)} %fusion.46), kind=kLoop, calls=%fused_computation.106 | loop fusion | flops 1048576 | bytes 3162112 | tf_op jit(solution)/shard_map/add | solution.py:84
  70.5 2.6 %select_compare_fusion = pred[4096]{0:T(1024)(128)(4,1)S(1)} fusion(pred[4096]{0:T(1024)(128)(4,1)S(1)} %copy-done.9, pred[4096]{0:T(1024)(128)(4,1)S(1)} %copy-done.8, pred[4096]{0:T(1024)(128)(4,1)S(1)} %copy-done.7, s32[]{:T(128)} %bitcast.5, s32[]{:T(128)} %bitcast.4, s32[]{:T(128)} %bitcast.3, s32[]{:T(128)} %bitcast.2), kind=kLoop, calls=%fused_computation.118 | loop fusion | flops 16384 | bytes 16400 | tf_op jit(solution)/shard_map/eq | solution.py:109
  77.6 29.7 %all-reduce.9 = (f32[48]{0:T(128)S(1)}, f32[48]{0:T(128)S(1)}, f32[16]{0:T(128)S(1)}) all-reduce(f32[48]{0:T(128)S(1)} %dynamic-update-slice.10, f32[48]{0:T(128)S(1)} %dynamic-update-slice.11, f32[16]{0:T(128)S(1)} %dynamic-update-slice.12), channel_id=2, replica_groups=mesh['win'=2,'row'=16] {'row'}, use_global_device_ids=true, to_apply=%add.6 | all-reduce | flops 112 | bytes 896
  107.5 19.4 %while.22 = (s32[]{:T(128)}, f32[3]{0:T(128)S(1)}, f32[3]{0:T(128)S(1)}, f32[1]{0:T(128)}, s32[]{:T(128)}, /*index=5*/f32[16,3]{1,0:T(8,128)S(1)}, f32[16,3]{1,0...) while((s32[]{:T(128)}, f32[3]{0:T(128)S(1)}, f32[3]{0:T(128)S(1)}, ...), condition=%wide.region_6.8_spmd.clone, body=%wide.region_5.7_spmd.clone.sunk | while | flops 25 | bytes 260 | solution.py:36
  127.0 1.9 collective-permute-start.4
  129.3 2.4 %broadcast_add_fusion = f32[3,64,4096]{2,1,0:T(8,128)S(1)} fusion(f32[3,64,4096]{2,1,0:T(8,128)} %param.18, f32[3,64]{1,0:T(4,128)S(1)} %subtract_add_fusion), kind=kLoop, calls=%fused_computation.104 | loop fusion | flops 786432 | bytes 6292224 | tf_op jit(solution)/shard_map/add | solution.py:144
  131.8 1.9 collective-permute-start.1
  133.7 4.2 %collective-permute-start.2 = (f32[3,1,4096]{2,1,0:T(1,128)S(1)}, f32[3,1,4096]{2,1,0:T(1,128)S(1)}, u32[]{:S(2)}, u32[]{:S(2)}) collective-permute-start(f32[3,1,4096]{2,1,0:T(1,128)S(1)} %get-tuple-element.257), channel_id=1, source_target_pairs={{1,0},{2,1},{3,2},{4,3},{5,4},{6,5},{7,6},{8,7},{9,8},{10,9},{11,1... | collective-permute-start | bytes 147464 | tf_op jit(solution)/shard_map/ppermute | solution.py:47
  137.9 2.3 %pad_maximum_fusion = f32[3,65,4096]{2,1,0:T(8,128)} fusion(f32[3,1,4096]{2,1,0:T(1,128)S(1)} %convert_element_type.42, f32[3,64,4096]{2,1,0:T(8,128)S(1)} %copy-done.3), kind=kLoop, calls=%fused_computation.13 | loop fusion | flops 798720 | bytes 6389760 | tf_op jit(solution)/shard_map/concatenate | solution.py:127
  140.3 2.3 %pad_maximum_fusion.1 = f32[3,65,4096]{2,1,0:T(8,128)} fusion(f32[3,1,4096]{2,1,0:T(1,128)S(1)} %convert_element_type.45, f32[3,64,4096]{2,1,0:T(8,128)S(1)} %scatter.6), kind=kLoop, calls=%fused_computation.15 | loop fusion | flops 798720 | bytes 6389760 | tf_op jit(solution)/shard_map/concatenate | solution.py:128
  143.9 10.5 %fusion.44 = (f32[3,64,4096]{2,1,0:T(8,128)S(1)}, f32[3,64,4096]{2,1,0:T(8,128)S(1)}) fusion(f32[3,66,4098]{2,1,0:T(8,128)S(1)} %select_maximum_fusion.6, f32[3,1,4096]{2,1,0:T(1,128)S(1)} %collective-permute-done.2, f32[3,64,4096]{2,1,0:T(8,128)S(1)} %broadcast_add_fusion, f32[3,1,4096]{2,1,0:T(1,128)S(1)} %collective-permute-done.1, ...), kind=kLoop, calls=%fused_computation.94 | loop fusion | flops 24379392 | bytes 43286528 | tf_op jit(solution)/shard_map/add | solution.py:83
  154.4 1.9 collective-permute-start.5
  156.4 2.7 %collective-permute-start.6 = (f32[3,1,4096]{2,1,0:T(1,128)S(1)}, f32[3,1,4096]{2,1,0:T(1,128)S(1)}, u32[]{:S(2)}, u32[]{:S(2)}) collective-permute-start(f32[3,1,4096]{2,1,0:T(1,128)S(1)} %get-tuple-element.255), channel_id=1, source_target_pairs={{1,0},{2,1},{3,2},{4,3},{5,4},{6,5},{7,6},{8,7},{9,8},{10,9},{11,1... | collective-permute-start | bytes 147464 | tf_op jit(solution)/shard_map/ppermute | solution.py:47
  159.1 3.0 %collective-permute-done.6 = f32[3,1,4096]{2,1,0:T(1,128)S(1)} collective-permute-done((f32[3,1,4096]{2,1,0:T(1,128)S(1)}, f32[3,1,4096]{2,1,0:T(1,128)S(1)}, u32[]{:S(2)}, u32[]{:S(2)}) %collective-permute-start.6) | collective-permute-done | bytes 49184 | tf_op jit(solution)/shard_map/ppermute | solution.py:47
  163.4 7.9 %fusion.36 = f32[3,64,4096]{2,1,0:T(8,128)} fusion(f32[3,64,4096]{2,1,0:T(8,128)S(1)} %get-tuple-element.245, f32[3,66,4098]{2,1,0:T(8,128)S(1)} %select_maximum_fusion.4, f32[3,1,4096]{2,1,0:T(1,128)S(1)} %collective-permute-done.6, f32[3,64,4096]{2,1,0:T(8,128)} %copy-done.1, f32[3,1,4096]{2,1,0:T(1,128)S(1)} %collective-permute-done.5, ...), kind=kLoop, calls=%fused_computation.79 | loop fusion | flops 14155776 | bytes 33653504 | tf_op jit(solution)/shard_map/add | solution.py:83
  172.5 1.9 collective-permute-start.7
  174.4 2.4 %collective-permute-start.8 = (f32[3,1,4096]{2,1,0:T(1,128)S(1)}, f32[3,1,4096]{2,1,0:T(1,128)S(1)}, u32[]{:S(2)}, u32[]{:S(2)}) collective-permute-start(f32[3,1,4096]{2,1,0:T(1,128)S(1)} %get-tuple-element.253), channel_id=1, source_target_pairs={{1,0},{2,1},{3,2},{4,3},{5,4},{6,5},{7,6},{8,7},{9,8},{10,9},{11,1... | collective-permute-start | bytes 147464 | tf_op jit(solution)/shard_map/ppermute | solution.py:47
  176.8 3.0 %collective-permute-done.8 = f32[3,1,4096]{2,1,0:T(1,128)S(1)} collective-permute-done((f32[3,1,4096]{2,1,0:T(1,128)S(1)}, f32[3,1,4096]{2,1,0:T(1,128)S(1)}, u32[]{:S(2)}, u32[]{:S(2)}) %collective-permute-start.8) | collective-permute-done | bytes 49184 | tf_op jit(solution)/shard_map/ppermute | solution.py:47
  179.8 3.1 %select_maximum_fusion.2 = f32[3,66,4098]{2,1,0:T(8,128)S(1)} fusion(f32[3,1,4096]{2,1,0:T(1,128)S(1)} %collective-permute-done.8, f32[3,64,4096]{2,1,0:T(8,128)} %fusion.36, f32[3,1,4096]{2,1,0:T(1,128)S(1)} %collective-permute-done.7), kind=kLoop, calls=%fused_computation.18 | loop fusion | flops 6491232 | bytes 6489648 | tf_op jit(solution)/shard_map/concatenate | solution.py:48
  182.9 8.1 %fusion.28 = f32[3,64,4096]{2,1,0:T(8,128)} fusion(f32[3,64,4096]{2,1,0:T(8,128)S(1)} %get-tuple-element.245, f32[3,66,4098]{2,1,0:T(8,128)S(1)} %select_maximum_fusion.2, f32[3,1,4096]{2,1,0:T(1,128)S(1)} %collective-permute-done.8, f32[3,64,4096]{2,1,0:T(8,128)} %fusion.36, f32[3,1,4096]{2,1,0:T(1,128)S(1)} %collective-permute-done.7, ...), kind=kLoop, calls=%fused_computation.64 | loop fusion | flops 14155776 | bytes 33653504 | tf_op jit(solution)/shard_map/add | solution.py:83
  194.2 2.6 %collective-permute-start.10 = (f32[3,1,4096]{2,1,0:T(1,128)S(1)}, f32[3,1,4096]{2,1,0:T(1,128)S(1)}, u32[]{:S(2)}, u32[]{:S(2)}) collective-permute-start(f32[3,1,4096]{2,1,0:T(1,128)S(1)} %get-tuple-element.251), channel_id=1, source_target_pairs={{1,0},{2,1},{3,2},{4,3},{5,4},{6,5},{7,6},{8,7},{9,8},{10,9},{11,1... | collective-permute-start | bytes 147464 | tf_op jit(solution)/shard_map/ppermute | solution.py:47
  196.8 2.8 %collective-permute-done.10 = f32[3,1,4096]{2,1,0:T(1,128)S(1)} collective-permute-done((f32[3,1,4096]{2,1,0:T(1,128)S(1)}, f32[3,1,4096]{2,1,0:T(1,128)S(1)}, u32[]{:S(2)}, u32[]{:S(2)}) %collective-permute-start.10) | collective-permute-done | bytes 49184 | tf_op jit(solution)/shard_map/ppermute | solution.py:47
  199.6 3.1 %select_maximum_fusion = f32[3,66,4098]{2,1,0:T(8,128)S(1)} fusion(f32[3,1,4096]{2,1,0:T(1,128)S(1)} %collective-permute-done.10, f32[3,64,4096]{2,1,0:T(8,128)} %fusion.28, f32[3,1,4096]{2,1,0:T(1,128)S(1)} %collective-permute-done.9), kind=kLoop, calls=%fused_computation.16 | loop fusion | flops 6491232 | bytes 6489648 | tf_op jit(solution)/shard_map/concatenate | solution.py:48
  202.7 7.9 %fusion.20 = f32[3,64,4096]{2,1,0:T(8,128)} fusion(f32[3,64,4096]{2,1,0:T(8,128)S(1)} %get-tuple-element.245, f32[3,66,4098]{2,1,0:T(8,128)S(1)} %select_maximum_fusion, f32[3,1,4096]{2,1,0:T(1,128)S(1)} %collective-permute-done.10, f32[3,64,4096]{2,1,0:T(8,128)} %fusion.28, f32[3,1,4096]{2,1,0:T(1,128)S(1)} %collective-permute-done.9, ...), kind=kLoop, calls=%fused_computation.49 | loop fusion | flops 14155776 | bytes 33653504 | tf_op jit(solution)/shard_map/add | solution.py:83
  (118 shorter events, 31.1 us)
Async XLA Ops:
  1.3 7.7 %copy-start.11 = (s32[4]{0:T(128)S(1)}, s32[4]{0:T(128)}, u32[]{:S(2)}) copy-start(s32[4]{0:T(128)} %constant.244.clone.1) | copy-start | bytes 52
  51.3 1.7 copy-start.2
  53.0 84.9 %collective-permute-start.3 = (bf16[3,1,4096]{2,1,0:T(2,128)(2,1)S(1)}, bf16[3,1,4096]{2,1,0:T(2,128)(2,1)S(1)}, u32[]{:S(2)}, u32[]{:S(2)}) collective-permute-start(bf16[3,1,4096]{2,1,0:T(2,128)(2,1)S(1)} %slice.552), channel_id=1, source_target_pairs={{0,1},{1,2},{2,3},{3,4},{4,5},{5,6},{6,7},{7,8},{8,9},{9,10},{10,1... | collective-permute-start | bytes 73736 | tf_op jit(solution)/shard_map/ppermute | solution.py:21
  59.3 2.5 %copy-start.12 = (s32[1,4,2]{1,2,0:T(2,128)S(1)}, s32[1,4,2]{1,2,0:T(2,128)}, u32[]{:S(2)}) copy-start(s32[1,4,2]{1,2,0:T(2,128)} %param.23) | copy-start | bytes 100
  59.3 5.4 %copy-start.10 = (s32[1,4]{1,0:T(1,128)S(1)}, s32[1,4]{1,0:T(1,128)}, u32[]{:S(2)}) copy-start(s32[1,4]{1,0:T(1,128)} %param.22) | copy-start | bytes 52
  59.3 6.0 %copy-start.7 = (pred[4096]{0:T(1024)(128)(4,1)S(1)}, pred[4096]{0:T(1024)(128)(4,1)}, u32[]{:S(2)}) copy-start(pred[4096]{0:T(1024)(128)(4,1)} %constant.303) | copy-start | bytes 12292
  59.3 6.0 %copy-start.8 = (pred[4096]{0:T(1024)(128)(4,1)S(1)}, pred[4096]{0:T(1024)(128)(4,1)}, u32[]{:S(2)}) copy-start(pred[4096]{0:T(1024)(128)(4,1)} %constant.302) | copy-start | bytes 12292
  59.3 5.9 %copy-start.9 = (pred[4096]{0:T(1024)(128)(4,1)S(1)}, pred[4096]{0:T(1024)(128)(4,1)}, u32[]{:S(2)}) copy-start(pred[4096]{0:T(1024)(128)(4,1)} %constant.301) | copy-start | bytes 12292
  59.9 16.6 %collective-permute-start = (bf16[3,4096]{1,0:T(4,128)(2,1)S(1)}, bf16[3,4096]{1,0:T(4,128)(2,1)S(1)}, u32[]{:S(2)}, u32[]{:S(2)}) collective-permute-start(bf16[3,4096]{1,0:T(4,128)(2,1)S(1)} %multiply_convert_fusion), channel_id=1, source_target_pairs={{1,0},{2,1},{3,2},{4,3},{5,4},{6,5},{7,6},{8,7},{9,8},{10,9},{11,1... | collective-permute-start | bytes 73736 | tf_op jit(solution)/shard_map/ppermute | solution.py:21
  62.5 11.8 %copy-start.13 = (u32[32]{0:T(128)S(1)}, u32[32]{0:T(128)}, u32[]{:S(2)}) copy-start(u32[32]{0:T(128)} %constant.284) | copy-start | bytes 388
  127.0 13.3 %collective-permute-start.4 = (bf16[3,1,4096]{2,1,0:T(2,128)(2,1)S(1)}, bf16[3,1,4096]{2,1,0:T(2,128)(2,1)S(1)}, u32[]{:S(2)}, u32[]{:S(2)}) collective-permute-start(bf16[3,1,4096]{2,1,0:T(2,128)(2,1)S(1)} %copy.33), channel_id=1, source_target_pairs={{0,1},{1,2},{2,3},{3,4},{4,5},{5,6},{6,7},{7,8},{8,9},{9,10},{10,1... | collective-permute-start | bytes 73736 | tf_op jit(solution)/shard_map/ppermute | solution.py:21
  129.3 8.7 %copy-start.3 = (f32[3,64,4096]{2,1,0:T(8,128)S(1)}, f32[3,64,4096]{2,1,0:T(8,128)}, u32[]{:S(2)}) copy-start(f32[3,64,4096]{2,1,0:T(8,128)} %copy-done.2) | copy-start | bytes 9437188
  131.8 10.9 %collective-permute-start.1 = (f32[3,1,4096]{2,1,0:T(1,128)S(1)}, f32[3,1,4096]{2,1,0:T(1,128)S(1)}, u32[]{:S(2)}, u32[]{:S(2)}) collective-permute-start(f32[3,1,4096]{2,1,0:T(1,128)S(1)} %get-tuple-element.256), channel_id=1, source_target_pairs={{0,1},{1,2},{2,3},{3,4},{4,5},{5,6},{6,7},{7,8},{8,9},{9,10},{10,1... | collective-permute-start | bytes 147464 | tf_op jit(solution)/shard_map/ppermute | solution.py:44
  133.7 8.9 %collective-permute-start.2 = (f32[3,1,4096]{2,1,0:T(1,128)S(1)}, f32[3,1,4096]{2,1,0:T(1,128)S(1)}, u32[]{:S(2)}, u32[]{:S(2)}) collective-permute-start(f32[3,1,4096]{2,1,0:T(1,128)S(1)} %get-tuple-element.257), channel_id=1, source_target_pairs={{1,0},{2,1},{3,2},{4,3},{5,4},{6,5},{7,6},{8,7},{9,8},{10,9},{11,1... | collective-permute-start | bytes 147464 | tf_op jit(solution)/shard_map/ppermute | solution.py:47
  142.6 1.3 copy-start.4
  154.3 9.0 %copy-start.1 = (f32[3,64,4096]{2,1,0:T(8,128)}, f32[3,64,4096]{2,1,0:T(8,128)S(1)}, u32[]{:S(2)}) copy-start(f32[3,64,4096]{2,1,0:T(8,128)S(1)} %get-tuple-element.244) | copy-start | bytes 9437188
  154.4 4.6 %collective-permute-start.5 = (f32[3,1,4096]{2,1,0:T(1,128)S(1)}, f32[3,1,4096]{2,1,0:T(1,128)S(1)}, u32[]{:S(2)}, u32[]{:S(2)}) collective-permute-start(f32[3,1,4096]{2,1,0:T(1,128)S(1)} %get-tuple-element.254), channel_id=1, source_target_pairs={{0,1},{1,2},{2,3},{3,4},{4,5},{5,6},{6,7},{7,8},{8,9},{9,10},{10,1... | collective-permute-start | bytes 147464 | tf_op jit(solution)/shard_map/ppermute | solution.py:44
  156.4 7.0 %copy-start = (f32[3,64,4096]{2,1,0:T(8,128)S(1)}, f32[3,64,4096]{2,1,0:T(8,128)}, u32[]{:S(2)}) copy-start(f32[3,64,4096]{2,1,0:T(8,128)} %param.18) | copy-start | bytes 9437188
  156.4 7.0 %copy-start.5 = (f32[64,4096]{1,0:T(8,128)S(1)}, f32[64,4096]{1,0:T(8,128)}, u32[]{:S(2)}) copy-start(f32[64,4096]{1,0:T(8,128)} %get-tuple-element.246) | copy-start | bytes 3145732
  156.4 7.0 %copy-start.6 = (f32[64,4096]{1,0:T(8,128)S(1)}, f32[64,4096]{1,0:T(8,128)}, u32[]{:S(2)}) copy-start(f32[64,4096]{1,0:T(8,128)} %get-tuple-element.247) | copy-start | bytes 3145732
  156.4 5.7 %collective-permute-start.6 = (f32[3,1,4096]{2,1,0:T(1,128)S(1)}, f32[3,1,4096]{2,1,0:T(1,128)S(1)}, u32[]{:S(2)}, u32[]{:S(2)}) collective-permute-start(f32[3,1,4096]{2,1,0:T(1,128)S(1)} %get-tuple-element.255), channel_id=1, source_target_pairs={{1,0},{2,1},{3,2},{4,3},{5,4},{6,5},{7,6},{8,7},{9,8},{10,9},{11,1... | collective-permute-start | bytes 147464 | tf_op jit(solution)/shard_map/ppermute | solution.py:47
  172.5 4.3 %collective-permute-start.7 = (f32[3,1,4096]{2,1,0:T(1,128)S(1)}, f32[3,1,4096]{2,1,0:T(1,128)S(1)}, u32[]{:S(2)}, u32[]{:S(2)}) collective-permute-start(f32[3,1,4096]{2,1,0:T(1,128)S(1)} %get-tuple-element.252), channel_id=1, source_target_pairs={{0,1},{1,2},{2,3},{3,4},{4,5},{5,6},{6,7},{7,8},{8,9},{9,10},{10,1... | collective-permute-start | bytes 147464 | tf_op jit(solution)/shard_map/ppermute | solution.py:44
  174.4 5.4 %collective-permute-start.8 = (f32[3,1,4096]{2,1,0:T(1,128)S(1)}, f32[3,1,4096]{2,1,0:T(1,128)S(1)}, u32[]{:S(2)}, u32[]{:S(2)}) collective-permute-start(f32[3,1,4096]{2,1,0:T(1,128)S(1)} %get-tuple-element.253), channel_id=1, source_target_pairs={{1,0},{2,1},{3,2},{4,3},{5,4},{6,5},{7,6},{8,7},{9,8},{10,9},{11,1... | collective-permute-start | bytes 147464 | tf_op jit(solution)/shard_map/ppermute | solution.py:47
  192.2 4.6 %collective-permute-start.9 = (f32[3,1,4096]{2,1,0:T(1,128)S(1)}, f32[3,1,4096]{2,1,0:T(1,128)S(1)}, u32[]{:S(2)}, u32[]{:S(2)}) collective-permute-start(f32[3,1,4096]{2,1,0:T(1,128)S(1)} %get-tuple-element.250), channel_id=1, source_target_pairs={{0,1},{1,2},{2,3},{3,4},{4,5},{5,6},{6,7},{7,8},{8,9},{9,10},{10,1... | collective-permute-start | bytes 147464 | tf_op jit(solution)/shard_map/ppermute | solution.py:44
  194.2 5.4 %collective-permute-start.10 = (f32[3,1,4096]{2,1,0:T(1,128)S(1)}, f32[3,1,4096]{2,1,0:T(1,128)S(1)}, u32[]{:S(2)}, u32[]{:S(2)}) collective-permute-start(f32[3,1,4096]{2,1,0:T(1,128)S(1)} %get-tuple-element.251), channel_id=1, source_target_pairs={{1,0},{2,1},{3,2},{4,3},{5,4},{6,5},{7,6},{8,7},{9,8},{10,9},{11,1... | collective-permute-start | bytes 147464 | tf_op jit(solution)/shard_map/ppermute | solution.py:47
where the time goes:
time: 212 us; the launch traced here: 211 us
  other arithmetic  70.1 us (33%)
  local copies, waits for them, and re-layouts  63.3 us (30%)
  blocking collectives  29.7 us (14%)
  starting transfers between devices  27.9 us (13%)
  loops' own time  9.62 us (5%)
  waiting for transfers between devices  8.76 us (4%)
    scatter x1, local copies, waits for them, and re-layouts, per_device(): horiz_tiles.at[:, :, :-1, TILE_COLS - 1]  34.4 us
    add x4, other arithmetic, relax(): (1.0 - OMEGA) * current  34.4 us
    unnamed x1, blocking collectives  29.7 us
    ppermute x4, starting transfers between devices, with_halo(): lax.ppermute(lax.slice_in_dim(block, 0, width, axis=dim), axis, backward)  11.9 us
    another operation x1, loops' own time, carried_in(): return lax.fori_loop(0, devices, turn, start)  9.62 us
    dynamic_slice x16, local copies, waits for them, and re-layouts, turn(): new = combine(before, jax.tree.map(lambda part: part[k], everything))  9.46 us
    ppermute x4, waiting for transfers between devices, with_halo(): lax.ppermute(lax.slice_in_dim(block, 0, width, axis=dim), axis, backward)  8.74 us
    concatenate x4, other arithmetic, with_halo(): block = jnp.concatenate([low, block, high], axis=dim)  8.71 us
  transfers between devices with their start and end apart: 11, of which 3 were waited for; matrix products, arithmetic and copies ran while one was open for 17% of the time, Pallas kernels for 0%

commit v1 on v0

--- a/solution.py
+++ b/solution.py
@@ -129,7 +129,9 @@
     )
     mean_vert = jnp.mean(vertical, axis=2)
     mean_image = jnp.mean(image, axis=2)
-    running = jnp.cumsum(mean_vert, axis=1) - mean_vert
+    above = jnp.arange(band_rows)
+    strictly = (above[None, :] < above[:, None]).astype(jnp.float32)
+    running = jnp.sum(strictly[None] * mean_vert[:, None, :], axis=2)
     totals = jnp.sum(mean_vert, axis=1)
     leading = mean_image[:, 0]
     empty_three = jnp.zeros((3,), jnp.float32)

time: 212 us -> 212 us (level)
  no operation moved by 1% of the time
where the time goes in v1:
time: 212 us; the launch traced here: 210 us
  other arithmetic  70 us (33%)
  local copies, waits for them, and re-layouts  63.3 us (30%)
  blocking collectives  29.7 us (14%)
  starting transfers between devices  27.9 us (13%)
  loops' own time  9.62 us (5%)
  waiting for transfers between devices  8.76 us (4%)
    scatter x1, local copies, waits for them, and re-layouts, per_device(): horiz_tiles.at[:, :, :-1, TILE_COLS - 1]  34.4 us
    add x4, other arithmetic, relax(): (1.0 - OMEGA) * current  34.4 us
    unnamed x1, blocking collectives  29.7 us
    ppermute x4, starting transfers between devices, with_halo(): lax.ppermute(lax.slice_in_dim(block, 0, width, axis=dim), axis, backward)  11.9 us
    another operation x1, loops' own time, carried_in(): return lax.fori_loop(0, devices, turn, start)  9.62 us
    dynamic_slice x16, local copies, waits for them, and re-layouts, turn(): new = combine(before, jax.tree.map(lambda part: part[k], everything))  9.46 us
    ppermute x4, waiting for transfers between devices, with_halo(): lax.ppermute(lax.slice_in_dim(block, 0, width, axis=dim), axis, backward)  8.74 us
    concatenate x4, other arithmetic, with_halo(): block = jnp.concatenate([low, block, high], axis=dim)  8.71 us
  transfers between devices with their start and end apart: 11, of which 3 were waited for; matrix products, arithmetic and copies ran while one was open for 17% of the time, Pallas kernels for 0%

profile of v1, /device:TPU:1, one launch (start us, length us, event | category | flops | bytes accessed | tf_op | source)
XLA Modules:
  0.0 210.5 jit_solution(460951785602453208)
XLA Ops:
  1.3 5.1 %reshape.228 = f32[3,64,4,1024]{3,2,1,0:T(4,128)} reshape(bf16[3,64,4096]{2,1,0:T(8,128)(2,1)} %param.19) | data formatting | bytes 4718592 | tf_op jit(solution)/shard_map/reshape | solution.py:113
  9.7 3.2 %dynamic-slice_select_fusion = f32[3,64,3,1]{3,2,1,0:T(4,128)S(1)} fusion(f32[3,64,4,1024]{3,2,1,0:T(4,128)} %reshape.228, s32[]{:T(128)} %bitcast.19, s32[]{:T(128)} %bitcast.20, f32[3,64,3,1]{3,2,1,0:T(4,128)S(1)} %copy.51, f32[3,64,3,1]{3,2,1,0:T(4,128)S(1)} %copy.52, pred[3]{0:T(512)(128)(4,1)S(1)} %compare_bitcast_fusion, pred[]{:T(512)} %and_reduce_fusion), kind=kLoop, calls=%fused_computation.109 | loop fusion | flops 1152 | bytes 9228 | tf_op jit(solution)/shard_map/select.6
  12.9 34.4 %scatter.9 = f32[3,64,4,1024]{3,2,1,0:T(4,128)} dynamic-update-slice(f32[3,64,4,1024]{3,2,1,0:T(4,128)} %reshape.228, f32[3,64,3,1]{3,2,1,0:T(4,128)S(1)} %dynamic-slice_select_fusion, s32[]{:T(128)} %constant.222.clone.1, s32[]{:T(128)} %constant.222.clone.1, s32[]{:T(128)} %bitcast.19, s32[]{:T(128)} %bitcast.20) | dynamic-update-slice | bytes 4612 | tf_op jit(solution)/shard_map/scatter | solution.py:117
  47.4 3.9 %reshape.226 = f32[3,64,4096]{2,1,0:T(8,128)S(1)} reshape(f32[3,64,4,1024]{3,2,1,0:T(4,128)} %scatter.9) | data formatting | bytes 6291456 | tf_op jit(solution)/shard_map/reshape | solution.py:120
  53.0 4.5 %collective-permute-start.3 = (bf16[3,1,4096]{2,1,0:T(2,128)(2,1)S(1)}, bf16[3,1,4096]{2,1,0:T(2,128)(2,1)S(1)}, u32[]{:S(2)}, u32[]{:S(2)}) collective-permute-start(bf16[3,1,4096]{2,1,0:T(2,128)(2,1)S(1)} %slice.552), channel_id=1, source_target_pairs={{0,1},{1,2},{2,3},{3,4},{4,5},{5,6},{6,7},{7,8},{8,9},{9,10},{10,1... | collective-permute-start | bytes 73736 | tf_op jit(solution)/shard_map/ppermute | solution.py:21
  59.9 1.9 collective-permute-start
  62.5 2.1 %reduce_sum.76 = f32[3,64]{1,0:T(4,128)S(1)} reduce(f32[3,64,4096]{2,1,0:T(8,128)} %param.18, f32[]{:T(128)} %constant.223.clone.1), dimensions={2}, to_apply=%region_4.6 | reduce | flops 786240 | bytes 3146500 | tf_op jit(solution)/shard_map/reduce_sum | solution.py:131
  65.3 2.5 %fusion.47 = f32[4096]{0:T(1024)S(1)} fusion(pred[4096]{0:T(1024)(128)(4,1)S(1)} %copy-done.9, pred[4096]{0:T(1024)(128)(4,1)S(1)} %copy-done.8, pred[4096]{0:T(1024)(128)(4,1)S(1)} %copy-done.7, s32[]{:T(128)} %bitcast.15, s32[]{:T(128)} %bitcast.14, s32[]{:T(128)} %bitcast.13, s32[]{:T(128)} %bitcast.12), kind=kLoop, calls=%fused_computation.120 | loop fusion | flops 20480 | bytes 28688 | tf_op jit(solution)/shard_map/mul | solution.py:152
  67.7 2.8 %broadcast_add_fusion.1 = (f32[64,4096]{1,0:T(8,128)}, f32[64,4096]{1,0:T(8,128)}) fusion(s32[64,4096]{1,0:T(8,128)} %param.21, f32[4096]{0:T(1024)S(1)} %fusion.47), kind=kLoop, calls=%fused_computation.106 | loop fusion | flops 1048576 | bytes 3162112 | tf_op jit(solution)/shard_map/add | solution.py:84
  70.6 2.6 %select_compare_fusion = pred[4096]{0:T(1024)(128)(4,1)S(1)} fusion(pred[4096]{0:T(1024)(128)(4,1)S(1)} %copy-done.9, pred[4096]{0:T(1024)(128)(4,1)S(1)} %copy-done.8, pred[4096]{0:T(1024)(128)(4,1)S(1)} %copy-done.7, s32[]{:T(128)} %bitcast.5, s32[]{:T(128)} %bitcast.4, s32[]{:T(128)} %bitcast.3, s32[]{:T(128)} %bitcast.2), kind=kLoop, calls=%fused_computation.121 | loop fusion | flops 16384 | bytes 16400 | tf_op jit(solution)/shard_map/eq | solution.py:109
  77.6 29.7 %all-reduce.9 = (f32[48]{0:T(128)S(1)}, f32[48]{0:T(128)S(1)}, f32[16]{0:T(128)S(1)}) all-reduce(f32[48]{0:T(128)S(1)} %dynamic-update-slice.10, f32[48]{0:T(128)S(1)} %dynamic-update-slice.11, f32[16]{0:T(128)S(1)} %dynamic-update-slice.12), channel_id=2, replica_groups=mesh['win'=2,'row'=16] {'row'}, use_global_device_ids=true, to_apply=%add.6 | all-reduce | flops 112 | bytes 896
  107.5 19.4 %while.22 = (s32[]{:T(128)}, f32[3]{0:T(128)S(1)}, f32[3]{0:T(128)S(1)}, f32[1]{0:T(128)}, s32[]{:T(128)}, /*index=5*/f32[16,3]{1,0:T(8,128)S(1)}, f32[16,3]{1,0...) while((s32[]{:T(128)}, f32[3]{0:T(128)S(1)}, f32[3]{0:T(128)S(1)}, ...), condition=%wide.region_6.8_spmd.clone, body=%wide.region_5.7_spmd.clone.sunk | while | flops 25 | bytes 260 | solution.py:36
  127.0 1.9 collective-permute-start.4
  129.1 2.4 %broadcast_add_fusion = f32[3,64,4096]{2,1,0:T(8,128)S(1)} fusion(f32[3,64,4096]{2,1,0:T(8,128)} %param.18, f32[3,64]{1,0:T(4,128)S(1)} %subtract_add_fusion), kind=kLoop, calls=%fused_computation.104 | loop fusion | flops 786432 | bytes 6292224 | tf_op jit(solution)/shard_map/add | solution.py:146
  131.6 1.9 collective-permute-start.1
  133.6 4.2 %collective-permute-start.2 = (f32[3,1,4096]{2,1,0:T(1,128)S(1)}, f32[3,1,4096]{2,1,0:T(1,128)S(1)}, u32[]{:S(2)}, u32[]{:S(2)}) collective-permute-start(f32[3,1,4096]{2,1,0:T(1,128)S(1)} %get-tuple-element.257), channel_id=1, source_target_pairs={{1,0},{2,1},{3,2},{4,3},{5,4},{6,5},{7,6},{8,7},{9,8},{10,9},{11,1... | collective-permute-start | bytes 147464 | tf_op jit(solution)/shard_map/ppermute | solution.py:47
  137.8 2.3 %pad_maximum_fusion = f32[3,65,4096]{2,1,0:T(8,128)} fusion(f32[3,1,4096]{2,1,0:T(1,128)S(1)} %convert_element_type.50, f32[3,64,4096]{2,1,0:T(8,128)S(1)} %copy-done.3), kind=kLoop, calls=%fused_computation.13 | loop fusion | flops 798720 | bytes 6389760 | tf_op jit(solution)/shard_map/concatenate | solution.py:127
  140.2 2.3 %pad_maximum_fusion.1 = f32[3,65,4096]{2,1,0:T(8,128)} fusion(f32[3,1,4096]{2,1,0:T(1,128)S(1)} %convert_element_type.53, f32[3,64,4096]{2,1,0:T(8,128)S(1)} %scatter.6), kind=kLoop, calls=%fused_computation.15 | loop fusion | flops 798720 | bytes 6389760 | tf_op jit(solution)/shard_map/concatenate | solution.py:128
  143.7 10.5 %fusion.44 = (f32[3,64,4096]{2,1,0:T(8,128)S(1)}, f32[3,64,4096]{2,1,0:T(8,128)S(1)}) fusion(f32[3,66,4098]{2,1,0:T(8,128)S(1)} %select_maximum_fusion.6, f32[3,1,4096]{2,1,0:T(1,128)S(1)} %collective-permute-done.2, f32[3,64,4096]{2,1,0:T(8,128)S(1)} %broadcast_add_fusion, f32[3,1,4096]{2,1,0:T(1,128)S(1)} %collective-permute-done.1, ...), kind=kLoop, calls=%fused_computation.94 | loop fusion | flops 24379392 | bytes 43286528 | tf_op jit(solution)/shard_map/add | solution.py:83
  154.3 1.9 collective-permute-start.5
  156.3 2.7 %collective-permute-start.6 = (f32[3,1,4096]{2,1,0:T(1,128)S(1)}, f32[3,1,4096]{2,1,0:T(1,128)S(1)}, u32[]{:S(2)}, u32[]{:S(2)}) collective-permute-start(f32[3,1,4096]{2,1,0:T(1,128)S(1)} %get-tuple-element.255), channel_id=1, source_target_pairs={{1,0},{2,1},{3,2},{4,3},{5,4},{6,5},{7,6},{8,7},{9,8},{10,9},{11,1... | collective-permute-start | bytes 147464 | tf_op jit(solution)/shard_map/ppermute | solution.py:47
  159.0 3.0 %collective-permute-done.6 = f32[3,1,4096]{2,1,0:T(1,128)S(1)} collective-permute-done((f32[3,1,4096]{2,1,0:T(1,128)S(1)}, f32[3,1,4096]{2,1,0:T(1,128)S(1)}, u32[]{:S(2)}, u32[]{:S(2)}) %collective-permute-start.6) | collective-permute-done | bytes 49184 | tf_op jit(solution)/shard_map/ppermute | solution.py:47
  163.2 7.9 %fusion.36 = f32[3,64,4096]{2,1,0:T(8,128)} fusion(f32[3,64,4096]{2,1,0:T(8,128)S(1)} %get-tuple-element.245, f32[3,66,4098]{2,1,0:T(8,128)S(1)} %select_maximum_fusion.4, f32[3,1,4096]{2,1,0:T(1,128)S(1)} %collective-permute-done.6, f32[3,64,4096]{2,1,0:T(8,128)} %copy-done.1, f32[3,1,4096]{2,1,0:T(1,128)S(1)} %collective-permute-done.5, ...), kind=kLoop, calls=%fused_computation.79 | loop fusion | flops 14155776 | bytes 33653504 | tf_op jit(solution)/shard_map/add | solution.py:83
  172.4 1.9 collective-permute-start.7
  174.3 2.4 %collective-permute-start.8 = (f32[3,1,4096]{2,1,0:T(1,128)S(1)}, f32[3,1,4096]{2,1,0:T(1,128)S(1)}, u32[]{:S(2)}, u32[]{:S(2)}) collective-permute-start(f32[3,1,4096]{2,1,0:T(1,128)S(1)} %get-tuple-element.253), channel_id=1, source_target_pairs={{1,0},{2,1},{3,2},{4,3},{5,4},{6,5},{7,6},{8,7},{9,8},{10,9},{11,1... | collective-permute-start | bytes 147464 | tf_op jit(solution)/shard_map/ppermute | solution.py:47
  176.7 3.0 %collective-permute-done.8 = f32[3,1,4096]{2,1,0:T(1,128)S(1)} collective-permute-done((f32[3,1,4096]{2,1,0:T(1,128)S(1)}, f32[3,1,4096]{2,1,0:T(1,128)S(1)}, u32[]{:S(2)}, u32[]{:S(2)}) %collective-permute-start.8) | collective-permute-done | bytes 49184 | tf_op jit(solution)/shard_map/ppermute | solution.py:47
  179.7 3.1 %select_maximum_fusion.2 = f32[3,66,4098]{2,1,0:T(8,128)S(1)} fusion(f32[3,1,4096]{2,1,0:T(1,128)S(1)} %collective-permute-done.8, f32[3,64,4096]{2,1,0:T(8,128)} %fusion.36, f32[3,1,4096]{2,1,0:T(1,128)S(1)} %collective-permute-done.7), kind=kLoop, calls=%fused_computation.18 | loop fusion | flops 6491232 | bytes 6489648 | tf_op jit(solution)/shard_map/concatenate | solution.py:48
  182.8 8.1 %fusion.28 = f32[3,64,4096]{2,1,0:T(8,128)} fusion(f32[3,64,4096]{2,1,0:T(8,128)S(1)} %get-tuple-element.245, f32[3,66,4098]{2,1,0:T(8,128)S(1)} %select_maximum_fusion.2, f32[3,1,4096]{2,1,0:T(1,128)S(1)} %collective-permute-done.8, f32[3,64,4096]{2,1,0:T(8,128)} %fusion.36, f32[3,1,4096]{2,1,0:T(1,128)S(1)} %collective-permute-done.7, ...), kind=kLoop, calls=%fused_computation.64 | loop fusion | flops 14155776 | bytes 33653504 | tf_op jit(solution)/shard_map/add | solution.py:83
  194.1 2.6 %collective-permute-start.10 = (f32[3,1,4096]{2,1,0:T(1,128)S(1)}, f32[3,1,4096]{2,1,0:T(1,128)S(1)}, u32[]{:S(2)}, u32[]{:S(2)}) collective-permute-start(f32[3,1,4096]{2,1,0:T(1,128)S(1)} %get-tuple-element.251), channel_id=1, source_target_pairs={{1,0},{2,1},{3,2},{4,3},{5,4},{6,5},{7,6},{8,7},{9,8},{10,9},{11,1... | collective-permute-start | bytes 147464 | tf_op jit(solution)/shard_map/ppermute | solution.py:47
  196.7 2.8 %collective-permute-done.10 = f32[3,1,4096]{2,1,0:T(1,128)S(1)} collective-permute-done((f32[3,1,4096]{2,1,0:T(1,128)S(1)}, f32[3,1,4096]{2,1,0:T(1,128)S(1)}, u32[]{:S(2)}, u32[]{:S(2)}) %collective-permute-start.10) | collective-permute-done | bytes 49184 | tf_op jit(solution)/shard_map/ppermute | solution.py:47
  199.5 3.1 %select_maximum_fusion = f32[3,66,4098]{2,1,0:T(8,128)S(1)} fusion(f32[3,1,4096]{2,1,0:T(1,128)S(1)} %collective-permute-done.10, f32[3,64,4096]{2,1,0:T(8,128)} %fusion.28, f32[3,1,4096]{2,1,0:T(1,128)S(1)} %collective-permute-done.9), kind=kLoop, calls=%fused_computation.16 | loop fusion | flops 6491232 | bytes 6489648 | tf_op jit(solution)/shard_map/concatenate | solution.py:48
  202.6 7.9 %fusion.20 = f32[3,64,4096]{2,1,0:T(8,128)} fusion(f32[3,64,4096]{2,1,0:T(8,128)S(1)} %get-tuple-element.245, f32[3,66,4098]{2,1,0:T(8,128)S(1)} %select_maximum_fusion, f32[3,1,4096]{2,1,0:T(1,128)S(1)} %collective-permute-done.10, f32[3,64,4096]{2,1,0:T(8,128)} %fusion.28, f32[3,1,4096]{2,1,0:T(1,128)S(1)} %collective-permute-done.9, ...), kind=kLoop, calls=%fused_computation.49 | loop fusion | flops 14155776 | bytes 33653504 | tf_op jit(solution)/shard_map/add | solution.py:83
  (119 shorter events, 31.0 us)
Async XLA Ops:
  1.3 7.7 %copy-start.11 = (s32[4]{0:T(128)S(1)}, s32[4]{0:T(128)}, u32[]{:S(2)}) copy-start(s32[4]{0:T(128)} %constant.241.clone.1) | copy-start | bytes 52
  51.3 1.7 copy-start.2
  53.0 84.8 %collective-permute-start.3 = (bf16[3,1,4096]{2,1,0:T(2,128)(2,1)S(1)}, bf16[3,1,4096]{2,1,0:T(2,128)(2,1)S(1)}, u32[]{:S(2)}, u32[]{:S(2)}) collective-permute-start(bf16[3,1,4096]{2,1,0:T(2,128)(2,1)S(1)} %slice.552), channel_id=1, source_target_pairs={{0,1},{1,2},{2,3},{3,4},{4,5},{5,6},{6,7},{7,8},{8,9},{9,10},{10,1... | collective-permute-start | bytes 73736 | tf_op jit(solution)/shard_map/ppermute | solution.py:21
  59.3 2.5 %copy-start.12 = (s32[1,4,2]{1,2,0:T(2,128)S(1)}, s32[1,4,2]{1,2,0:T(2,128)}, u32[]{:S(2)}) copy-start(s32[1,4,2]{1,2,0:T(2,128)} %param.23) | copy-start | bytes 100
  59.3 5.4 %copy-start.10 = (s32[1,4]{1,0:T(1,128)S(1)}, s32[1,4]{1,0:T(1,128)}, u32[]{:S(2)}) copy-start(s32[1,4]{1,0:T(1,128)} %param.22) | copy-start | bytes 52
  59.3 6.0 %copy-start.7 = (pred[4096]{0:T(1024)(128)(4,1)S(1)}, pred[4096]{0:T(1024)(128)(4,1)}, u32[]{:S(2)}) copy-start(pred[4096]{0:T(1024)(128)(4,1)} %constant.300) | copy-start | bytes 12292
  59.3 6.0 %copy-start.8 = (pred[4096]{0:T(1024)(128)(4,1)S(1)}, pred[4096]{0:T(1024)(128)(4,1)}, u32[]{:S(2)}) copy-start(pred[4096]{0:T(1024)(128)(4,1)} %constant.299) | copy-start | bytes 12292
  59.3 6.0 %copy-start.9 = (pred[4096]{0:T(1024)(128)(4,1)S(1)}, pred[4096]{0:T(1024)(128)(4,1)}, u32[]{:S(2)}) copy-start(pred[4096]{0:T(1024)(128)(4,1)} %constant.298) | copy-start | bytes 12292
  59.9 16.7 %collective-permute-start = (bf16[3,4096]{1,0:T(4,128)(2,1)S(1)}, bf16[3,4096]{1,0:T(4,128)(2,1)S(1)}, u32[]{:S(2)}, u32[]{:S(2)}) collective-permute-start(bf16[3,4096]{1,0:T(4,128)(2,1)S(1)} %multiply_convert_fusion), channel_id=1, source_target_pairs={{1,0},{2,1},{3,2},{4,3},{5,4},{6,5},{7,6},{8,7},{9,8},{10,9},{11,1... | collective-permute-start | bytes 73736 | tf_op jit(solution)/shard_map/ppermute | solution.py:21
  62.5 11.8 %copy-start.13 = (u32[32]{0:T(128)S(1)}, u32[32]{0:T(128)}, u32[]{:S(2)}) copy-start(u32[32]{0:T(128)} %constant.281) | copy-start | bytes 388
  127.0 13.1 %collective-permute-start.4 = (bf16[3,1,4096]{2,1,0:T(2,128)(2,1)S(1)}, bf16[3,1,4096]{2,1,0:T(2,128)(2,1)S(1)}, u32[]{:S(2)}, u32[]{:S(2)}) collective-permute-start(bf16[3,1,4096]{2,1,0:T(2,128)(2,1)S(1)} %copy.53), channel_id=1, source_target_pairs={{0,1},{1,2},{2,3},{3,4},{4,5},{5,6},{6,7},{7,8},{8,9},{9,10},{10,1... | collective-permute-start | bytes 73736 | tf_op jit(solution)/shard_map/ppermute | solution.py:21
  129.1 8.7 %copy-start.3 = (f32[3,64,4096]{2,1,0:T(8,128)S(1)}, f32[3,64,4096]{2,1,0:T(8,128)}, u32[]{:S(2)}) copy-start(f32[3,64,4096]{2,1,0:T(8,128)} %copy-done.2) | copy-start | bytes 9437188
  131.6 10.9 %collective-permute-start.1 = (f32[3,1,4096]{2,1,0:T(1,128)S(1)}, f32[3,1,4096]{2,1,0:T(1,128)S(1)}, u32[]{:S(2)}, u32[]{:S(2)}) collective-permute-start(f32[3,1,4096]{2,1,0:T(1,128)S(1)} %get-tuple-element.256), channel_id=1, source_target_pairs={{0,1},{1,2},{2,3},{3,4},{4,5},{5,6},{6,7},{7,8},{8,9},{9,10},{10,1... | collective-permute-start | bytes 147464 | tf_op jit(solution)/shard_map/ppermute | solution.py:44
  133.6 8.9 %collective-permute-start.2 = (f32[3,1,4096]{2,1,0:T(1,128)S(1)}, f32[3,1,4096]{2,1,0:T(1,128)S(1)}, u32[]{:S(2)}, u32[]{:S(2)}) collective-permute-start(f32[3,1,4096]{2,1,0:T(1,128)S(1)} %get-tuple-element.257), channel_id=1, source_target_pairs={{1,0},{2,1},{3,2},{4,3},{5,4},{6,5},{7,6},{8,7},{9,8},{10,9},{11,1... | collective-permute-start | bytes 147464 | tf_op jit(solution)/shard_map/ppermute | solution.py:47
  142.5 1.3 copy-start.4
  154.2 9.0 %copy-start.1 = (f32[3,64,4096]{2,1,0:T(8,128)}, f32[3,64,4096]{2,1,0:T(8,128)S(1)}, u32[]{:S(2)}) copy-start(f32[3,64,4096]{2,1,0:T(8,128)S(1)} %get-tuple-element.244) | copy-start | bytes 9437188
  154.3 4.6 %collective-permute-start.5 = (f32[3,1,4096]{2,1,0:T(1,128)S(1)}, f32[3,1,4096]{2,1,0:T(1,128)S(1)}, u32[]{:S(2)}, u32[]{:S(2)}) collective-permute-start(f32[3,1,4096]{2,1,0:T(1,128)S(1)} %get-tuple-element.254), channel_id=1, source_target_pairs={{0,1},{1,2},{2,3},{3,4},{4,5},{5,6},{6,7},{7,8},{8,9},{9,10},{10,1... | collective-permute-start | bytes 147464 | tf_op jit(solution)/shard_map/ppermute | solution.py:44
  156.2 7.0 %copy-start = (f32[3,64,4096]{2,1,0:T(8,128)S(1)}, f32[3,64,4096]{2,1,0:T(8,128)}, u32[]{:S(2)}) copy-start(f32[3,64,4096]{2,1,0:T(8,128)} %param.18) | copy-start | bytes 9437188
  156.3 7.0 %copy-start.5 = (f32[64,4096]{1,0:T(8,128)S(1)}, f32[64,4096]{1,0:T(8,128)}, u32[]{:S(2)}) copy-start(f32[64,4096]{1,0:T(8,128)} %get-tuple-element.246) | copy-start | bytes 3145732
  156.3 7.0 %copy-start.6 = (f32[64,4096]{1,0:T(8,128)S(1)}, f32[64,4096]{1,0:T(8,128)}, u32[]{:S(2)}) copy-start(f32[64,4096]{1,0:T(8,128)} %get-tuple-element.247) | copy-start | bytes 3145732
  156.3 5.7 %collective-permute-start.6 = (f32[3,1,4096]{2,1,0:T(1,128)S(1)}, f32[3,1,4096]{2,1,0:T(1,128)S(1)}, u32[]{:S(2)}, u32[]{:S(2)}) collective-permute-start(f32[3,1,4096]{2,1,0:T(1,128)S(1)} %get-tuple-element.255), channel_id=1, source_target_pairs={{1,0},{2,1},{3,2},{4,3},{5,4},{6,5},{7,6},{8,7},{9,8},{10,9},{11,1... | collective-permute-start | bytes 147464 | tf_op jit(solution)/shard_map/ppermute | solution.py:47
  172.4 4.3 %collective-permute-start.7 = (f32[3,1,4096]{2,1,0:T(1,128)S(1)}, f32[3,1,4096]{2,1,0:T(1,128)S(1)}, u32[]{:S(2)}, u32[]{:S(2)}) collective-permute-start(f32[3,1,4096]{2,1,0:T(1,128)S(1)} %get-tuple-element.252), channel_id=1, source_target_pairs={{0,1},{1,2},{2,3},{3,4},{4,5},{5,6},{6,7},{7,8},{8,9},{9,10},{10,1... | collective-permute-start | bytes 147464 | tf_op jit(solution)/shard_map/ppermute | solution.py:44
  174.3 5.4 %collective-permute-start.8 = (f32[3,1,4096]{2,1,0:T(1,128)S(1)}, f32[3,1,4096]{2,1,0:T(1,128)S(1)}, u32[]{:S(2)}, u32[]{:S(2)}) collective-permute-start(f32[3,1,4096]{2,1,0:T(1,128)S(1)} %get-tuple-element.253), channel_id=1, source_target_pairs={{1,0},{2,1},{3,2},{4,3},{5,4},{6,5},{7,6},{8,7},{9,8},{10,9},{11,1... | collective-permute-start | bytes 147464 | tf_op jit(solution)/shard_map/ppermute | solution.py:47
  192.1 4.6 %collective-permute-start.9 = (f32[3,1,4096]{2,1,0:T(1,128)S(1)}, f32[3,1,4096]{2,1,0:T(1,128)S(1)}, u32[]{:S(2)}, u32[]{:S(2)}) collective-permute-start(f32[3,1,4096]{2,1,0:T(1,128)S(1)} %get-tuple-element.250), channel_id=1, source_target_pairs={{0,1},{1,2},{2,3},{3,4},{4,5},{5,6},{6,7},{7,8},{8,9},{9,10},{10,1... | collective-permute-start | bytes 147464 | tf_op jit(solution)/shard_map/ppermute | solution.py:44
  194.1 5.4 %collective-permute-start.10 = (f32[3,1,4096]{2,1,0:T(1,128)S(1)}, f32[3,1,4096]{2,1,0:T(1,128)S(1)}, u32[]{:S(2)}, u32[]{:S(2)}) collective-permute-start(f32[3,1,4096]{2,1,0:T(1,128)S(1)} %get-tuple-element.251), channel_id=1, source_target_pairs={{1,0},{2,1},{3,2},{4,3},{5,4},{6,5},{7,6},{8,7},{9,8},{10,9},{11,1... | collective-permute-start | bytes 147464 | tf_op jit(solution)/shard_map/ppermute | solution.py:47

commit v2 on v0

v2 whole, which is shorter than its diff:
```python
import functools

import jax
import jax.numpy as jnp
from jax import lax
from jax.experimental import pallas as pl
from jax.experimental.pallas import tpu as pltpu
from jax.sharding import PartitionSpec as P

TILE_ROWS = 1024
TILE_COLS = 1024
BAND = 48
SWEEPS = 4
OMEGA = 0.8
SCREEN = 0.25
LANES = 128
SUB = 8
PAD = 8
MESH = pl.DeviceIdType.MESH


def kernel(
    n, image, grad_x, grad_y, classes, validity, owners, out,
    s, a_term, b_term, gxf, gyf, sums, level, tot, gathered, band_out, band_in,
    halo_send, halo_recv, grad_send, grad_recv, tot_send, tot_recv, band_sems,
):
    channels, rows, width = image.shape
    blocks, tiles = width // LANES, rows // SUB
    per_tile = TILE_COLS // LANES
    seams_below = validity.shape[0] > 1
    pos = lax.axis_index("row")
    win = lax.axis_index("win")
    tile_row = pos * rows // TILE_ROWS
    lane = lax.broadcasted_iota(jnp.int32, (SUB, LANES), 1)
    lane16 = lax.broadcasted_iota(jnp.int32, (2 * SUB, LANES), 1)
    first_lane, last_lane = lane == 0, lane == LANES - 1
    zero = jnp.zeros((SUB, LANES), jnp.float32)
    has_above, has_below = pos > 0, pos < n - 1

    barrier = pltpu.get_barrier_semaphore()

    def greet(j, carry):
        @pl.when((j < pos) | (j == pos + 1))
        def _():
            pl.semaphore_signal(barrier, inc=1, device_id=(win, j), device_id_type=MESH)
        return carry

    lax.fori_loop(0, n, greet, 0)

    def remote(src, dst, send, recv, to):
        return pltpu.make_async_remote_copy(
            src_ref=src, dst_ref=dst, send_sem=send, recv_sem=recv,
            device_id=(win, to), device_id_type=MESH,
        )

    def row_of(ref, row):
        return ref.at[:, :, pl.ds(row, 1), :]

    def gy_pass(j, carry):
        k, at = j // (tiles // 2), (j % (tiles // 2)) * 2 * SUB
        total = [None, None]
        for c in range(blocks):
            v = grad_y[k, pl.ds(at, 2 * SUB), c * LANES:(c + 1) * LANES].astype(jnp.float32)
            gyf[k, c, pl.ds(PAD + at, 2 * SUB), :] = v
            total[c % 2] = v if total[c % 2] is None else total[c % 2] + v
        sums[0, k, pl.ds(at, 2 * SUB), :] = total[0] + total[1]
        return carry

    lax.fori_loop(0, channels * tiles // 2, gy_pass, 0)

    def gx_pass(j, carry):
        k, at = j // (tiles // 2), (j % (tiles // 2)) * 2 * SUB
        for c in range(blocks):
            v = grad_x[k, pl.ds(at, 2 * SUB), c * LANES:(c + 1) * LANES].astype(jnp.float32)
            if (c + 1) % per_tile == 0 and c + 1 < blocks:
                after = grad_x[k, pl.ds(at, 2 * SUB), (c + 1) * LANES:(c + 2) * LANES].astype(jnp.float32)
                inside = (lane16 >= LANES - 1 - BAND) & (lane16 < LANES - 1)
                left = jnp.sum(jnp.where(inside, v, 0.0), axis=1, keepdims=True)
                right = jnp.sum(jnp.where(lane16 < BAND, after, 0.0), axis=1, keepdims=True)
                owns = owners[tile_row, c // per_tile, 1] == 1
                mean = jnp.where(owns, right, left) * (1.0 / BAND)
                v = jnp.where(lane16 == LANES - 1, mean, v)
            gxf[k, c, pl.ds(PAD + at, 2 * SUB), :] = v
        return carry

    lax.fori_loop(0, channels * tiles // 2, gx_pass, 0)

    pl.semaphore_wait(barrier, n - 1 - pos + jnp.where(has_above, 1, 0))

    if seams_below:
        def band_pass(j, carry):
            k, c = j // blocks, j % blocks
            mean = jnp.sum(gyf[k, c, PAD:PAD + BAND, :], axis=0, keepdims=True) * (1.0 / BAND)
            band_out[k, c] = jnp.broadcast_to(mean, (SUB, LANES))
            return carry

        lax.fori_loop(0, channels * blocks, band_pass, 0)
        band = remote(row_of(band_out, 0), row_of(band_in, 0), band_sems.at[0], band_sems.at[1], pos - 1)

        @pl.when(has_above)
        def _():
            band.start()

        @pl.when(has_below)
        def _():
            band.wait_recv()

        @pl.when(has_above)
        def _():
            band.wait_send()

        at_seam = has_below & ((pos + 1) * rows % TILE_ROWS == 0)

        @pl.when(at_seam)
        def _():
            last = PAD + rows - 1
            for k in range(channels):
                total = jnp.zeros((1, LANES), jnp.float32)
                for c in range(blocks):
                    upper = jnp.sum(gyf[k, c, last - BAND:last, :], axis=0, keepdims=True) * (1.0 / BAND)
                    owns = owners[tile_row, c // per_tile, 0] == 1
                    new = jnp.where(owns, band_in[k, c, 0:1, :], upper)
                    gyf[k, c, last:last + 1, :] = new
                    total = total + new
                sums[0, k, rows - 1:rows, :] = total

    grads = [
        remote(row_of(g, PAD + rows - 1), row_of(g, PAD - 1), grad_send.at[q], grad_recv.at[q], pos + 1)
        for q, g in enumerate((gxf, gyf))
    ]

    @pl.when(has_below)
    def _():
        for copy in grads:
            copy.start()

    tot[...] = zero
    for k in range(channels):
        first = image[k, 0:SUB, 0:LANES]
        for c in range(1, blocks):
            first = first + image[k, 0:SUB, c * LANES:(c + 1) * LANES]
        mean = jnp.sum(first, axis=1, keepdims=True) * (1.0 / width)
        tot[channels + k:channels + k + 1, :] = jnp.broadcast_to(mean[0:1], (1, LANES))
        my = jnp.sum(sums[0, k], axis=1, keepdims=True) * (1.0 / width)
        sums[0, k] = jnp.broadcast_to(my, (rows, LANES))
        tot[k:k + 1, :] = jnp.broadcast_to(jnp.sum(my, axis=0, keepdims=True), (1, LANES))

    def tell(j, carry):
        @pl.when(j > pos)
        def _():
            remote(tot, gathered.at[pos], tot_send.at[j], tot_recv.at[pos], j).start()
        return carry

    lax.fori_loop(0, n, tell, 0)

    @pl.when(jnp.logical_not(has_above))
    def _():
        for k in range(channels):
            for c in range(blocks):
                gxf[k, c, PAD - 1:PAD, :] = zero[:1]
                gyf[k, c, PAD - 1:PAD, :] = zero[:1]
                for t in range(SWEEPS):
                    s[t, k, c, PAD - 1:PAD, :] = zero[:1]

    @pl.when(jnp.logical_not(has_below))
    def _():
        for k in range(channels):
            for c in range(blocks):
                for t in range(SWEEPS):
                    s[t, k, c, PAD + rows:PAD + rows + 1, :] = zero[:1]

    def image_pass(j, carry):
        k, at = j // tiles, (j % tiles) * SUB
        total = [None, None]
        for c in range(blocks):
            v = image[k, pl.ds(at, SUB), c * LANES:(c + 1) * LANES]
            total[c % 2] = v if total[c % 2] is None else total[c % 2] + v
        sums[1, k, pl.ds(at, SUB), :] = total[0] + total[1]
        return carry

    lax.fori_loop(0, channels * tiles, image_pass, 0)

    def weight_pass(i, carry):
        at = i * SUB
        for c in range(blocks):
            power = (1 << classes[pl.ds(at, SUB), c * LANES:(c + 1) * LANES]).astype(jnp.float32)
            cover = validity[tile_row, c // per_tile].astype(jnp.float32) * SCREEN
            b_term[c, pl.ds(at, SUB), :] = OMEGA / (cover * power + 6.0)
        return carry

    lax.fori_loop(0, tiles, weight_pass, 0)

    def div_tile(k, i):
        at = i * SUB
        state = []

        def load(c):
            x0, xm = gxf[k, c, pl.ds(PAD + at, SUB), :], gxf[k, c, pl.ds(PAD - 1 + at, SUB), :]
            y0, ym = gyf[k, c, pl.ds(PAD + at, SUB), :], gyf[k, c, pl.ds(PAD - 1 + at, SUB), :]
            x = 1.5 * x0 + 0.5 * xm
            y = 0.5 * y0
            return x + y0 - 2.0 * ym, pltpu.roll(y - x, 1, 1), pltpu.roll(y, LANES - 1, 1)

        before, here = zero, load(0)
        for c in range(blocks):
            after = load(c + 1) if c + 1 < blocks else (None, None, zero)
            base, left, right = here
            moved = jnp.where(first_lane, before, left) + jnp.where(last_lane, after[2], right)
            a_term[k, c, pl.ds(at, SUB), :] = b_term[c, pl.ds(at, SUB), :] * (base + moved)
            before, here = left, after

    def div_loop(j, carry):
        div_tile(j // (tiles - 1), 1 + j % (tiles - 1))
        return carry

    lax.fori_loop(0, channels * (tiles - 1), div_loop, 0)

    @pl.when(has_above)
    def _():
        for copy in grads:
            copy.wait_recv()

    def div_first(k, carry):
        div_tile(k, 0)
        return carry

    lax.fori_loop(0, channels, div_first, 0)

    down = lax.broadcasted_iota(jnp.int32, (rows, rows), 0)
    across = lax.broadcasted_iota(jnp.int32, (rows, rows), 1)
    strictly = (across < down).astype(jnp.float32)
    for k in range(channels):
        running = jnp.dot(
            strictly, sums[0, k], precision=lax.Precision.HIGHEST, preferred_element_type=jnp.float32
        )
        mf = jnp.sum(sums[1, k], axis=1, keepdims=True) * (1.0 / width)
        level[k] = running - mf

    gathered[pos] = tot[...]

    def hear(j, carry):
        @pl.when(j < pos)
        def _():
            remote(tot, gathered.at[j], tot_send.at[j], tot_recv.at[j], j).wait_recv()
        return carry

    lax.fori_loop(0, n, hear, 0)
    before = lax.fori_loop(0, pos, lambda j, total: total + gathered[j], zero)
    leading = gathered[0]
    for k in range(channels):
        level[k] = level[k] + (before[k:k + 1, :] + leading[channels + k:channels + k + 1, :])

    def start_tile(k, i):
        at = i * SUB
        up = level[k, pl.ds(at, SUB), :]
        for c in range(blocks):
            target = image[k, pl.ds(at, SUB), c * LANES:(c + 1) * LANES] + up
            s[0, k, c, pl.ds(PAD + at, SUB), :] = target
            rest = OMEGA - 6.0 * b_term[c, pl.ds(at, SUB), :]
            a_term[k, c, pl.ds(at, SUB), :] = rest * target - a_term[k, c, pl.ds(at, SUB), :]

    def sweep_tile(t, k, i):
        at = i * SUB

        def load(c):
            mid = s[t, k, c, pl.ds(PAD + at, SUB), :]
            v = s[t, k, c, pl.ds(PAD - 1 + at, SUB), :] + s[t, k, c, pl.ds(PAD + 1 + at, SUB), :]
            q = mid + 0.5 * v
            return mid, v, pltpu.roll(q, 1, 1), pltpu.roll(q, LANES - 1, 1)

        before, here = zero, load(0)
        for c in range(blocks):
            after = load(c + 1) if c + 1 < blocks else (None, None, None, zero)
            mid, v, left, right = here
            around = v + jnp.where(first_lane, before, left) + jnp.where(last_lane, after[3], right)
            new = (1.0 - OMEGA) * mid + (
                a_term[k, c, pl.ds(at, SUB), :] + b_term[c, pl.ds(at, SUB), :] * around
            )
            if t + 1 < SWEEPS:
                s[t + 1, k, c, pl.ds(PAD + at, SUB), :] = new
            else:
                out[k, pl.ds(at, SUB), c * LANES:(c + 1) * LANES] = new
            before, here = left, after

    def halo(t):
        up = remote(row_of(s.at[t], PAD), row_of(s.at[t], PAD + rows), halo_send.at[t, 0], halo_recv.at[t, 0], pos - 1)
        dn = remote(row_of(s.at[t], PAD + rows - 1), row_of(s.at[t], PAD - 1), halo_send.at[t, 1], halo_recv.at[t, 1], pos + 1)
        return up, dn

    def rim_then_inner(work, t):
        def rim(j, carry):
            work(j // 2, (j % 2) * (tiles - 1))
            return carry

        def inner(j, carry):
            work(j // (tiles - 2), 1 + j % (tiles - 2))
            return carry

        lax.fori_loop(0, channels * 2, rim, 0)
        if t < SWEEPS:
            up, dn = halo(t)

            @pl.when(has_above)
            def _():
                up.start()

            @pl.when(has_below)
            def _():
                dn.start()

        lax.fori_loop(0, channels * (tiles - 2), inner, 0)
        if t < SWEEPS:
            @pl.when(has_below)
            def _():
                up.wait_recv()

            @pl.when(has_above)
            def _():
                dn.wait_recv()

    rim_then_inner(start_tile, 0)
    for t in range(SWEEPS):
        rim_then_inner(functools.partial(sweep_tile, t), t + 1)

    for t in range(SWEEPS):
        up, dn = halo(t)

        @pl.when(has_above)
        def _():
            up.wait_send()

        @pl.when(has_below)
        def _():
            dn.wait_send()

    @pl.when(has_below)
    def _():
        for copy in grads:
            copy.wait_send()

    def sent(j, carry):
        @pl.when(j > pos)
        def _():
            remote(tot, gathered.at[pos], tot_send.at[j], tot_recv.at[pos], j).wait_send()
        return carry

    lax.fori_loop(0, n, sent, 0)


def per_device(image, grad_x, grad_y, classes, validity, owners):
    n = lax.axis_size("row")
    channels, rows, width = image.shape
    blocks = width // LANES
    vmem, smem = pl.BlockSpec(memory_space=pltpu.VMEM), pl.BlockSpec(memory_space=pltpu.SMEM)
    f32 = jnp.float32
    band_rows = SUB if validity.shape[0] > 1 else 1
    band_blocks = blocks if validity.shape[0] > 1 else 1
    return pl.pallas_call(
        functools.partial(kernel, n),
        out_shape=jax.ShapeDtypeStruct(image.shape, f32),
        in_specs=[vmem] * 4 + [smem] * 2,
        out_specs=vmem,
        scratch_shapes=[
            pltpu.VMEM((SWEEPS, channels, blocks, PAD + rows + SUB, LANES), f32),
            pltpu.VMEM((channels, blocks, rows, LANES), f32),
            pltpu.VMEM((blocks, rows, LANES), f32),
            pltpu.VMEM((channels, blocks, PAD + rows, LANES), f32),
            pltpu.VMEM((channels, blocks, PAD + rows, LANES), f32),
            pltpu.VMEM((2, channels, rows, LANES), f32),
            pltpu.VMEM((channels, rows, LANES), f32),
            pltpu.VMEM((SUB, LANES), f32),
            pltpu.VMEM((n, SUB, LANES), f32),
            pltpu.VMEM((channels, band_blocks, band_rows, LANES), f32),
            pltpu.VMEM((channels, band_blocks, band_rows, LANES), f32),
            pltpu.SemaphoreType.DMA((SWEEPS, 2)),
            pltpu.SemaphoreType.DMA((SWEEPS, 2)),
            pltpu.SemaphoreType.DMA((2,)),
            pltpu.SemaphoreType.DMA((2,)),
            pltpu.SemaphoreType.DMA((n,)),
            pltpu.SemaphoreType.DMA((n,)),
            pltpu.SemaphoreType.DMA((2,)),
        ],
        compiler_params=pltpu.CompilerParams(
            collective_id=0, has_side_effects=True, vmem_limit_bytes=56 * 2**20
        ),
    )(image, grad_x, grad_y, classes, validity, owners)


def solution(mesh):
    in_specs = (
        P(None, ("win", "row"), None),
        P(None, ("win", "row"), None),
        P(None, ("win", "row"), None),
        P(("win", "row"), None),
        P("win", None),
        P("win", None, None),
    )
    out_specs = P(None, ("win", "row"), None)
    return jax.shard_map(
        per_device, mesh=mesh, in_specs=in_specs, out_specs=out_specs, check_vma=False
    )
```

time: 212 us -> 39 us (0.18)
  other arithmetic: 70.1 us -> 0 us
  local copies, waits for them, and re-layouts: 63.3 us -> 5.19 us
  Pallas kernels: 0 us -> 33.6 us
  blocking collectives: 29.7 us -> 0 us
  starting transfers between devices: 27.9 us -> 0 us
  loops' own time: 9.62 us -> 0 us
  waiting for transfers between devices: 8.76 us -> 0 us
    add x7 -> x0, other arithmetic: 39.7 us -> none  [the longest x4 34.4 us: relax(): (1.0 - OMEGA) * current]
    scatter x2 -> x0, local copies, waits for them, and re-layouts: 34.8 us -> none  [the longest x1 34.4 us: per_device(): horiz_tiles.at[:, :, :-1, TILE_COLS - 1]]
    pallas_call x0 -> x1, Pallas kernels: none -> 33.6 us  [per_device(): pl.pallas_call(functools.partial(kernel, n), out_shape=jax.ShapeDtypeStru...]
    unnamed x1 -> x0, blocking collectives: 29.7 us -> none
    ppermute x11 -> x0, starting transfers between devices: 27.9 us -> none  [the longest x4 11.9 us: with_halo(): lax.ppermute(lax.slice_in_dim(block, 0, width, axis=dim), axis, backward)]
    concatenate x6 -> x0, other arithmetic: 13.3 us -> none  [the longest x4 8.71 us: with_halo(): block = jnp.concatenate([low, block, high], axis=dim)]
    another operation x1 -> x0, loops' own time: 9.62 us -> none  [carried_in(): return lax.fori_loop(0, devices, turn, start)]
    dynamic_slice x16 -> x0, local copies, waits for them, and re-layouts: 9.46 us -> none  [turn(): new = combine(before, jax.tree.map(lambda part: part[k], everything))]
  transfers between devices with their start and end apart: 11 -> 0, of which waited for: 3 -> 0; matrix products, arithmetic and copies ran while one was open for 17% -> 0% of each run, Pallas kernels for 0% -> 0%
where the time goes in v2:
time: 39 us; the launch traced here: 38.8 us
  Pallas kernels  33.6 us (86%)
  local copies, waits for them, and re-layouts  5.19 us (13%)
    pallas_call x1, Pallas kernels, per_device(): pl.pallas_call(functools.partial(kernel, n), out_shape=jax.ShapeDtypeStru...  33.6 us
    unnamed x2, local copies, waits for them, and re-layouts  5.19 us

profile of v2, /device:TPU:1, one launch (start us, length us, event | category | flops | bytes accessed | tf_op | source)
XLA Modules:
  0.0 38.8 jit_solution(17989681167617525045)
XLA Ops:
  0.0 1.3 %copy.7.owners = s32[1,4,2]{2,1,0:T(4,128)} copy(s32[1,4,2]{1,2,0:T(2,128)} %param.11) | data formatting | bytes 64 | tf_op args[5]
  1.3 33.6 %shard_map.64 = f32[3,64,4096]{2,1,0:T(8,128)} custom-call(f32[3,64,4096]{2,1,0:T(8,128)} %image.1, bf16[3,64,4096]{2,1,0:T(8,128)(2,1)} %grad_x.1, bf16[3,64,4096]{2,1,0:T(8,128)(2,1)} %grad_y.1, s32[64,4096]{1,0:T(8,128)} %classes.1, s32[1,4]{1,0:T(1,128)} %validity.1, s32[1,4,2]{2,1,0:T(4,128)} %copy.7.owners), custom_call_target="tpu_custom_call" | custom-call | tf_op jit(solution)/shard_map/pallas_call | solution.py:358
  35.0 3.9 %copy.9 = f32[3,64,4096]{2,1,0:T(8,128)} copy(f32[3,64,4096]{2,1,0:T(8,128)} %shard_map.64) | data formatting | bytes 6291456

commit v3 on v2

--- a/solution.py
+++ b/solution.py
@@ -20,11 +20,11 @@
 
 
 def kernel(
-    n, image, grad_x, grad_y, classes, validity, owners, out,
-    s, a_term, b_term, gxf, gyf, sums, level, tot, gathered, band_out, band_in,
-    halo_send, halo_recv, grad_send, grad_recv, tot_send, tot_recv, band_sems,
+    n, image_in, gx_in, gy_in, classes_in, validity, owners, out,
+    image, grad_x, grad_y, classes, s0, s1, s2, s3, d_term, a_term, b_term, gxf, gyf, sums, level, tot, gathered, band_out, band_in,
+    halo_send, halo_recv, grad_send, grad_recv, tot_send, tot_recv, band_sems, in_sems,
 ):
-    channels, rows, width = image.shape
+    channels, rows, width = image_in.shape
     blocks, tiles = width // LANES, rows // SUB
     per_tile = TILE_COLS // LANES
     seams_below = validity.shape[0] > 1
@@ -37,6 +37,16 @@
     zero = jnp.zeros((SUB, LANES), jnp.float32)
     has_above, has_below = pos > 0, pos < n - 1
 
+    iterates = (s0, s1, s2, s3)
+    fetch_gy, fetch_gx, fetch_image, fetch_classes = (
+        pltpu.make_async_copy(src, dst, in_sems.at[q])
+        for q, (src, dst) in enumerate(
+            ((gy_in, grad_y), (gx_in, grad_x), (image_in, image), (classes_in, classes))
+        )
+    )
+    for fetch in (fetch_gy, fetch_gx, fetch_image, fetch_classes):
+        fetch.start()
+
     barrier = pltpu.get_barrier_semaphore()
 
     def greet(j, carry):
@@ -66,6 +76,7 @@
         sums[0, k, pl.ds(at, 2 * SUB), :] = total[0] + total[1]
         return carry
 
+    fetch_gy.wait()
     lax.fori_loop(0, channels * tiles // 2, gy_pass, 0)
 
     def gx_pass(j, carry):
@@ -77,12 +88,13 @@
                 inside = (lane16 >= LANES - 1 - BAND) & (lane16 < LANES - 1)
                 left = jnp.sum(jnp.where(inside, v, 0.0), axis=1, keepdims=True)
                 right = jnp.sum(jnp.where(lane16 < BAND, after, 0.0), axis=1, keepdims=True)
-                owns = owners[tile_row, c // per_tile, 1] == 1
+                owns = owners[tile_row, 1, c // per_tile] == 1
                 mean = jnp.where(owns, right, left) * (1.0 / BAND)
                 v = jnp.where(lane16 == LANES - 1, mean, v)
             gxf[k, c, pl.ds(PAD + at, 2 * SUB), :] = v
         return carry
 
+    fetch_gx.wait()
     lax.fori_loop(0, channels * tiles // 2, gx_pass, 0)
 
     pl.semaphore_wait(barrier, n - 1 - pos + jnp.where(has_above, 1, 0))
@@ -118,7 +130,7 @@
                 total = jnp.zeros((1, LANES), jnp.float32)
                 for c in range(blocks):
                     upper = jnp.sum(gyf[k, c, last - BAND:last, :], axis=0, keepdims=True) * (1.0 / BAND)
-                    owns = owners[tile_row, c // per_tile, 0] == 1
+                    owns = owners[tile_row, 0, c // per_tile] == 1
                     new = jnp.where(owns, band_in[k, c, 0:1, :], upper)
                     gyf[k, c, last:last + 1, :] = new
                     total = total + new
@@ -134,6 +146,7 @@
         for copy in grads:
             copy.start()
 
+    fetch_image.wait()
     tot[...] = zero
     for k in range(channels):
         first = image[k, 0:SUB, 0:LANES]
@@ -160,14 +173,14 @@
                 gxf[k, c, PAD - 1:PAD, :] = zero[:1]
                 gyf[k, c, PAD - 1:PAD, :] = zero[:1]
                 for t in range(SWEEPS):
-                    s[t, k, c, PAD - 1:PAD, :] = zero[:1]
+                    iterates[t][k, c, PAD - 1:PAD, :] = zero[:1]
 
     @pl.when(jnp.logical_not(has_below))
     def _():
         for k in range(channels):
             for c in range(blocks):
                 for t in range(SWEEPS):
-                    s[t, k, c, PAD + rows:PAD + rows + 1, :] = zero[:1]
+                    iterates[t][k, c, PAD + rows:PAD + rows + 1, :] = zero[:1]
 
     def image_pass(j, carry):
         k, at = j // tiles, (j % tiles) * SUB
@@ -188,6 +201,7 @@
             b_term[c, pl.ds(at, SUB), :] = OMEGA / (cover * power + 6.0)
         return carry
 
+    fetch_classes.wait()
     lax.fori_loop(0, tiles, weight_pass, 0)
 
     def div_tile(k, i):
@@ -206,7 +220,7 @@
             after = load(c + 1) if c + 1 < blocks else (None, None, zero)
             base, left, right = here
             moved = jnp.where(first_lane, before, left) + jnp.where(last_lane, after[2], right)
-            a_term[k, c, pl.ds(at, SUB), :] = b_term[c, pl.ds(at, SUB), :] * (base + moved)
+            d_term[k, c, pl.ds(at, SUB), :] = b_term[c, pl.ds(at, SUB), :] * (base + moved)
             before, here = left, after
 
     def div_loop(j, carry):
@@ -255,16 +269,16 @@
         up = level[k, pl.ds(at, SUB), :]
         for c in range(blocks):
             target = image[k, pl.ds(at, SUB), c * LANES:(c + 1) * LANES] + up
-            s[0, k, c, pl.ds(PAD + at, SUB), :] = target
+            s0[k, c, pl.ds(PAD + at, SUB), :] = target
             rest = OMEGA - 6.0 * b_term[c, pl.ds(at, SUB), :]
-            a_term[k, c, pl.ds(at, SUB), :] = rest * target - a_term[k, c, pl.ds(at, SUB), :]
+            a_term[k, c, pl.ds(at, SUB), :] = rest * target - d_term[k, c, pl.ds(at, SUB), :]
 
     def sweep_tile(t, k, i):
         at = i * SUB
 
         def load(c):
-            mid = s[t, k, c, pl.ds(PAD + at, SUB), :]
-            v = s[t, k, c, pl.ds(PAD - 1 + at, SUB), :] + s[t, k, c, pl.ds(PAD + 1 + at, SUB), :]
+            mid = iterates[t][k, c, pl.ds(PAD + at, SUB), :]
+            v = iterates[t][k, c, pl.ds(PAD - 1 + at, SUB), :] + iterates[t][k, c, pl.ds(PAD + 1 + at, SUB), :]
             q = mid + 0.5 * v
             return mid, v, pltpu.roll(q, 1, 1), pltpu.roll(q, LANES - 1, 1)
 
@@ -277,14 +291,14 @@
                 a_term[k, c, pl.ds(at, SUB), :] + b_term[c, pl.ds(at, SUB), :] * around
             )
             if t + 1 < SWEEPS:
-                s[t + 1, k, c, pl.ds(PAD + at, SUB), :] = new
+                iterates[t + 1][k, c, pl.ds(PAD + at, SUB), :] = new
             else:
                 out[k, pl.ds(at, SUB), c * LANES:(c + 1) * LANES] = new
             before, here = left, after
 
     def halo(t):
-        up = remote(row_of(s.at[t], PAD), row_of(s.at[t], PAD + rows), halo_send.at[t, 0], halo_recv.at[t, 0], pos - 1)
-        dn = remote(row_of(s.at[t], PAD + rows - 1), row_of(s.at[t], PAD - 1), halo_send.at[t, 1], halo_recv.at[t, 1], pos + 1)
+        up = remote(row_of(iterates[t], PAD), row_of(iterates[t], PAD + rows), halo_send.at[t, 0], halo_recv.at[t, 0], pos - 1)
+        dn = remote(row_of(iterates[t], PAD + rows - 1), row_of(iterates[t], PAD - 1), halo_send.at[t, 1], halo_recv.at[t, 1], pos + 1)
         return up, dn
 
     def rim_then_inner(work, t):
@@ -357,11 +371,16 @@
     band_blocks = blocks if validity.shape[0] > 1 else 1
     return pl.pallas_call(
         functools.partial(kernel, n),
-        out_shape=jax.ShapeDtypeStruct(image.shape, f32),
-        in_specs=[vmem] * 4 + [smem] * 2,
+        out_shape=pltpu.VMEM(image.shape, f32),
+        in_specs=[pl.BlockSpec(memory_space=pl.ANY)] * 4 + [smem] * 2,
         out_specs=vmem,
         scratch_shapes=[
-            pltpu.VMEM((SWEEPS, channels, blocks, PAD + rows + SUB, LANES), f32),
+            pltpu.VMEM(image.shape, image.dtype),
+            pltpu.VMEM(grad_x.shape, grad_x.dtype),
+            pltpu.VMEM(grad_y.shape, grad_y.dtype),
+            pltpu.VMEM(classes.shape, classes.dtype),
+            *[pltpu.VMEM((channels, blocks, PAD + rows + SUB, LANES), f32)] * SWEEPS,
+            pltpu.VMEM((channels, blocks, rows, LANES), f32),
             pltpu.VMEM((channels, blocks, rows, LANES), f32),
             pltpu.VMEM((blocks, rows, LANES), f32),
             pltpu.VMEM((channels, blocks, PAD + rows, LANES), f32),
@@ -379,11 +398,12 @@
             pltpu.SemaphoreType.DMA((n,)),
             pltpu.SemaphoreType.DMA((n,)),
             pltpu.SemaphoreType.DMA((2,)),
+            pltpu.SemaphoreType.DMA((4,)),
         ],
         compiler_params=pltpu.CompilerParams(
-            collective_id=0, has_side_effects=True, vmem_limit_bytes=56 * 2**20
+            collective_id=0, has_side_effects=True, vmem_limit_bytes=50 * 2**20
         ),
-    )(image, grad_x, grad_y, classes, validity, owners)
+    )(image, grad_x, grad_y, classes, validity, jnp.swapaxes(owners, 1, 2))
 
 
 def solution(mesh):

time: 39 us -> 32.6 us (0.84)
  Pallas kernels: 33.6 us -> 29.4 us
  local copies, waits for them, and re-layouts: 5.19 us -> 3 us
    pallas_call x1, Pallas kernels: 33.6 us -> 29.4 us  [per_device(): pl.pallas_call(functools.partial(kernel, n), out_shape=pltpu.VMEM(image.s...]
    unnamed x2 -> x5, local copies, waits for them, and re-layouts: 5.19 us -> 3 us
where the time goes in v3:
time: 32.6 us; the launch traced here: 32.4 us
  Pallas kernels  29.4 us (90%)
  local copies, waits for them, and re-layouts  3 us (9%)
    pallas_call x1, Pallas kernels, per_device(): pl.pallas_call(functools.partial(kernel, n), out_shape=pltpu.VMEM(image.s...  29.4 us
    unnamed x5, local copies, waits for them, and re-layouts  3 us

profile of v3, /device:TPU:1, one launch (start us, length us, event | category | flops | bytes accessed | tf_op | source)
XLA Modules:
  0.0 32.4 jit_solution(17915635118647079276)
XLA Ops:
  0.0 0.0 copy-start
  0.0 0.7 %copy-done = s32[1,4,2]{1,2,0:T(2,128)S(1)} copy-done((s32[1,4,2]{1,2,0:T(2,128)S(1)}, s32[1,4,2]{1,2,0:T(2,128)}, u32[]{:S(2)}) %copy-start) | copy-done | bytes 56
  0.7 0.0 copy-start.1
  0.7 0.7 %copy-done.1 = s32[1,4]{1,0:T(1,128)S(1)} copy-done((s32[1,4]{1,0:T(1,128)S(1)}, s32[1,4]{1,0:T(1,128)}, u32[]{:S(2)}) %copy-start.1) | copy-done | bytes 40
  1.3 29.4 %shard_map.64 = f32[3,64,4096]{2,1,0:T(8,128)S(1)} custom-call(f32[3,64,4096]{2,1,0:T(8,128)} %image_in.1, bf16[3,64,4096]{2,1,0:T(8,128)(2,1)} %gx_in.1, bf16[3,64,4096]{2,1,0:T(8,128)(2,1)} %gy_in.1, s32[64,4096]{1,0:T(8,128)} %classes_in.1, s32[1,4]{1,0:T(1,128)S(1)} %copy-done.1, s32[1,2,4]{2,1,0:T(2,128)S(1)} %bitcast.1), custom_call_target="tpu_custom_call" | custom-call | tf_op jit(solution)/shard_map/pallas_call | solution.py:372
  30.7 1.7 %copy.8 = f32[3,64,4096]{2,1,0:T(8,128)} copy(f32[3,64,4096]{2,1,0:T(8,128)S(1)} %shard_map.64) | data formatting | bytes 6291456
Async XLA Ops:
  0.0 0.7 %copy-start = (s32[1,4,2]{1,2,0:T(2,128)S(1)}, s32[1,4,2]{1,2,0:T(2,128)}, u32[]{:S(2)}) copy-start(s32[1,4,2]{1,2,0:T(2,128)} %param.11) | copy-start | bytes 100
  0.7 0.7 %copy-start.1 = (s32[1,4]{1,0:T(1,128)S(1)}, s32[1,4]{1,0:T(1,128)}, u32[]{:S(2)}) copy-start(s32[1,4]{1,0:T(1,128)} %validity.1) | copy-start | bytes 52

commit v4 on v3

--- a/solution.py
+++ b/solution.py
@@ -17,6 +17,7 @@
 SUB = 8
 PAD = 8
 MESH = pl.DeviceIdType.MESH
+AHEAD = 6
 
 
 def kernel(
@@ -215,13 +216,16 @@
             y = 0.5 * y0
             return x + y0 - 2.0 * ym, pltpu.roll(y - x, 1, 1), pltpu.roll(y, LANES - 1, 1)
 
-        before, here = zero, load(0)
-        for c in range(blocks):
-            after = load(c + 1) if c + 1 < blocks else (None, None, zero)
+        before, ready = zero, [load(c) for c in range(min(AHEAD, blocks))]
+        for c in range(blocks):
+            if c + AHEAD < blocks:
+                ready.append(load(c + AHEAD))
+            here = ready.pop(0)
+            after = ready[0] if ready else (None, None, zero)
             base, left, right = here
             moved = jnp.where(first_lane, before, left) + jnp.where(last_lane, after[2], right)
             d_term[k, c, pl.ds(at, SUB), :] = b_term[c, pl.ds(at, SUB), :] * (base + moved)
-            before, here = left, after
+            before = left
 
     def div_loop(j, carry):
         div_tile(j // (tiles - 1), 1 + j % (tiles - 1))
@@ -282,9 +286,12 @@
             q = mid + 0.5 * v
             return mid, v, pltpu.roll(q, 1, 1), pltpu.roll(q, LANES - 1, 1)
 
-        before, here = zero, load(0)
-        for c in range(blocks):
-            after = load(c + 1) if c + 1 < blocks else (None, None, None, zero)
+        before, ready = zero, [load(c) for c in range(min(AHEAD, blocks))]
+        for c in range(blocks):
+            if c + AHEAD < blocks:
+                ready.append(load(c + AHEAD))
+            here = ready.pop(0)
+            after = ready[0] if ready else (None, None, None, zero)
             mid, v, left, right = here
             around = v + jnp.where(first_lane, before, left) + jnp.where(last_lane, after[3], right)
             new = (1.0 - OMEGA) * mid + (
@@ -294,7 +301,7 @@
                 iterates[t + 1][k, c, pl.ds(PAD + at, SUB), :] = new
             else:
                 out[k, pl.ds(at, SUB), c * LANES:(c + 1) * LANES] = new
-            before, here = left, after
+            before = left
 
     def halo(t):
         up = remote(row_of(iterates[t], PAD), row_of(iterates[t], PAD + rows), halo_send.at[t, 0], halo_recv.at[t, 0], pos - 1)

time: 32.6 us -> 32.6 us (level)
  no operation moved by 1% of the time
where the time goes in v4:
time: 32.6 us; the launch traced here: 32.4 us
  Pallas kernels  29.4 us (90%)
  local copies, waits for them, and re-layouts  3 us (9%)
    pallas_call x1, Pallas kernels, per_device(): pl.pallas_call(functools.partial(kernel, n), out_shape=pltpu.VMEM(image.s...  29.4 us
    unnamed x5, local copies, waits for them, and re-layouts  3 us

profile of v4, /device:TPU:1, one launch (start us, length us, event | category | flops | bytes accessed | tf_op | source)
XLA Modules:
  0.0 32.4 jit_solution(17915635118647079276)
XLA Ops:
  0.0 0.0 copy-start
  0.0 0.7 %copy-done = s32[1,4,2]{1,2,0:T(2,128)S(1)} copy-done((s32[1,4,2]{1,2,0:T(2,128)S(1)}, s32[1,4,2]{1,2,0:T(2,128)}, u32[]{:S(2)}) %copy-start) | copy-done | bytes 56
  0.7 0.0 copy-start.1
  0.7 0.7 %copy-done.1 = s32[1,4]{1,0:T(1,128)S(1)} copy-done((s32[1,4]{1,0:T(1,128)S(1)}, s32[1,4]{1,0:T(1,128)}, u32[]{:S(2)}) %copy-start.1) | copy-done | bytes 40
  1.3 29.4 %shard_map.64 = f32[3,64,4096]{2,1,0:T(8,128)S(1)} custom-call(f32[3,64,4096]{2,1,0:T(8,128)} %image_in.1, bf16[3,64,4096]{2,1,0:T(8,128)(2,1)} %gx_in.1, bf16[3,64,4096]{2,1,0:T(8,128)(2,1)} %gy_in.1, s32[64,4096]{1,0:T(8,128)} %classes_in.1, s32[1,4]{1,0:T(1,128)S(1)} %copy-done.1, s32[1,2,4]{2,1,0:T(2,128)S(1)} %bitcast.1), custom_call_target="tpu_custom_call" | custom-call | tf_op jit(solution)/shard_map/pallas_call | solution.py:379
  30.7 1.7 %copy.8 = f32[3,64,4096]{2,1,0:T(8,128)} copy(f32[3,64,4096]{2,1,0:T(8,128)S(1)} %shard_map.64) | data formatting | bytes 6291456
Async XLA Ops:
  0.0 0.7 %copy-start = (s32[1,4,2]{1,2,0:T(2,128)S(1)}, s32[1,4,2]{1,2,0:T(2,128)}, u32[]{:S(2)}) copy-start(s32[1,4,2]{1,2,0:T(2,128)} %param.11) | copy-start | bytes 100
  0.7 0.7 %copy-start.1 = (s32[1,4]{1,0:T(1,128)S(1)}, s32[1,4]{1,0:T(1,128)}, u32[]{:S(2)}) copy-start(s32[1,4]{1,0:T(1,128)} %validity.1) | copy-start | bytes 52
